TPU v7x, 128 devices: a whole 4x4x4 slice. The times are simulated.
128 devices in a mesh: seq: 32 (over y, x, core), head: 4 (over z).
Axes of the slice: x: 4, y: 4, z: 4, core: 2. Of those that a mesh axis runs over, the one named last changes fastest.
Arguments:
- queries: bfloat16 [4096, 128, 576], P('seq', 'head'), may hold values from -51 to 51
- cache: bfloat16 [4096, 576], P(('seq', 'head')), may hold values from -6 to 6
- lists: int32 [64, 15], P('seq'), may hold values from -1 to 62, as said below
- w_uv: bfloat16 [128, 512, 128], P('head'), may hold values from -0.25 to 0.25
- grad_out: bfloat16 [4096, 128, 128], P('seq', 'head'), may hold values from -6 to 6
Outputs:
- head_out: bfloat16 [4096, 128, 128], P('seq', 'head')
- grad_queries: bfloat16 [4096, 128, 576], P('seq', 'head')
- grad_cache: float32 [4096, 576], P(('seq', 'head'))
- grad_uv: bfloat16 [128, 512, 128], P('head')
Inputs may be any that keep to these rules, and one draw needn't show every extreme that they name: `lists`: -1 marks an empty entry. Any other entry of row g names a block of a lower sequence shard than block g's, or a block of the same shard before g, at most once in the row. The rows of one sequence shard together name at most 1 distinct blocks of any one shard's 128 // 64 blocks, and exactly 1 in some draw pair.
All inputs are finite; a program needn't handle non-finite values.
Results may differ from a plain program's by a relative error of at most 0.015.
Values may be sent and summed in bfloat16 or wider, within the bound.
A program may use at most 192 MiB of HBM per device.

v0:
```python
import jax
import jax.numpy as jnp
from jax import lax
from jax.sharding import PartitionSpec as P

D_LAT = 512
BLK = 64
KEEP = 15


score_scale = 192.0 ** (-0.5)


def key_mask(entries):
    row_pos = jnp.arange(BLK)[:, None]
    col_pos = jnp.arange((KEEP + 1) * BLK)[None, :]
    slot_pos = col_pos // BLK
    present = jnp.concatenate([jnp.array([True]), entries >= 0])
    return jnp.where(slot_pos == 0, col_pos <= row_pos, present[slot_pos])


def block_pass(query_rows, key_rows, valid, grad_rows, weight):
    value_rows = key_rows[:, :D_LAT]
    scores = (
        jnp.einsum("rhk,ck->hrc", query_rows, key_rows, preferred_element_type=jnp.float32)
        * score_scale
    )
    scores = jnp.where(valid[None], scores, -jnp.inf)
    top_score = jnp.max(scores, axis=-1, keepdims=True)
    expo = jnp.exp(scores - top_score)
    probs = (expo / jnp.sum(expo, axis=-1, keepdims=True)).astype(jnp.bfloat16)
    latent_out = jnp.einsum(
        "hrc,cd->rhd", probs, value_rows, preferred_element_type=jnp.float32
    ).astype(jnp.bfloat16)
    output = jnp.einsum(
        "rhd,hde->rhe", latent_out, weight, preferred_element_type=jnp.float32
    ).astype(jnp.bfloat16)
    grad_latent = jnp.einsum(
        "rhe,hde->rhd", grad_rows, weight, preferred_element_type=jnp.float32
    ).astype(jnp.bfloat16)
    weight_term = jnp.einsum(
        "rhd,rhe->hde", latent_out, grad_rows, preferred_element_type=jnp.float32
    )
    grad_probs = jnp.einsum(
        "rhd,cd->hrc", grad_latent, value_rows, preferred_element_type=jnp.float32
    )
    probs_f = probs.astype(jnp.float32)
    centre = jnp.sum(probs_f * grad_probs, axis=-1, keepdims=True)
    grad_scores = (score_scale * probs_f * (grad_probs - centre)).astype(jnp.bfloat16)
    grad_query = jnp.einsum(
        "hrc,ck->rhk", grad_scores, key_rows, preferred_element_type=jnp.float32
    ).astype(jnp.bfloat16)
    grad_keys = jnp.einsum(
        "hrc,rhk->ck", grad_scores, query_rows, preferred_element_type=jnp.float32
    )
    grad_values = jnp.einsum("hrc,rhd->cd", probs, grad_latent, preferred_element_type=jnp.float32)
    grad_keys = grad_keys.at[:, :D_LAT].add(grad_values)
    return (output, grad_query, grad_keys, weight_term)


def on_device(queries, cache, lists, w_uv, grad_out):
    local_cache = lax.all_gather(cache, "head", axis=0, tiled=True)
    tok_dev = queries.shape[0]
    per_dev = tok_dev // BLK
    kv_width = cache.shape[1]
    first_block = lax.axis_index("seq") * per_dev
    own_blocks = local_cache.reshape(per_dev, BLK, kv_width)
    safe_lists = jnp.maximum(lists, 0)
    whole = lax.all_gather(local_cache, "seq", axis=0, tiled=True)
    source = whole.reshape(-1, BLK, kv_width)

    def step(carry, index):
        grad_source, grad_own, grad_weight = carry
        entries = lists[index]
        slot_row = safe_lists[index]
        key_rows = jnp.concatenate([own_blocks[index][None], source[slot_row]], 0).reshape(
            -1, kv_width
        )
        query_rows = lax.dynamic_slice_in_dim(queries, index * BLK, BLK, 0)
        grad_rows = lax.dynamic_slice_in_dim(grad_out, index * BLK, BLK, 0)
        output, grad_query, grad_keys, weight_term = block_pass(
            query_rows, key_rows, key_mask(entries), grad_rows, w_uv
        )
        grad_keys = grad_keys.reshape(KEEP + 1, BLK, kv_width)
        grad_source = grad_source.at[slot_row].add(grad_keys[1:])
        grad_own = grad_own.at[index].add(grad_keys[0])
        return ((grad_source, grad_own, grad_weight + weight_term), (output, grad_query))

    init = (
        jnp.zeros(source.shape, jnp.float32),
        jnp.zeros((per_dev, BLK, kv_width), jnp.float32),
        jnp.zeros(w_uv.shape, jnp.float32),
    )
    (grad_source, grad_own, grad_weight), (outputs, grad_queries) = lax.scan(
        step, init, jnp.arange(per_dev, dtype=jnp.int32)
    )
    full_grad = grad_source.reshape(-1, kv_width)
    own_rows = lax.dynamic_slice_in_dim(
        full_grad, first_block * BLK, tok_dev, 0
    ) + grad_own.reshape(tok_dev, kv_width)
    full_grad = lax.dynamic_update_slice_in_dim(full_grad, own_rows, first_block * BLK, 0)
    grad_cache = lax.psum_scatter(full_grad, ("seq", "head"), scatter_dimension=0, tiled=True)
    grad_uv = lax.psum(grad_weight, "seq").astype(jnp.bfloat16)
    head_out = outputs.reshape(tok_dev, outputs.shape[2], outputs.shape[3])
    grad_q = grad_queries.reshape(tok_dev, grad_queries.shape[2], grad_queries.shape[3])
    return (head_out, grad_q, grad_cache, grad_uv)


def solution(mesh):
    return jax.shard_map(
        on_device,
        mesh=mesh,
        in_specs=(
            P("seq", "head", None),
            P(("seq", "head"), None),
            P("seq", None),
            P("head", None, None),
            P("seq", "head", None),
        ),
        out_specs=(
            P("seq", "head", None),
            P("seq", "head", None),
            P(("seq", "head"), None),
            P("head", None, None),
        ),
        check_vma=False,
    )
```

profile of v0, /device:TPU:1, one launch (start us, length us, event | category | flops | bytes accessed | tf_op | source)
XLA Modules:
  0.0 896.1 jit_solution(18074344952866980986)
XLA Ops:
  7.2 13.4 %all_gather.6 = bf16[128,576]{1,0:T(8,128)(2,1)} all-gather(bf16[32,576]{1,0:T(8,128)(2,1)} %param.13), channel_id=1, replica_groups=mesh['seq'=32,'head'=4] {'head'}, dimensions={0}, use_global_device_ids=true | all-gather | bytes 184320 | tf_op jit(solution)/shard_map/all_gather | solution.py:62
  20.8 7.6 copy.24
  28.4 43.0 %all-gather.2.cloned.1.call-done = bf16[4096,576]{1,0:T(8,128)(2,1)} async-done(((bf16[128,576]{1,0:T(8,128)(2,1)}), bf16[4096,576]{1,0:T(8,128)(2,1)}) %all-gather.2.cloned.1.call-update) | async-done | bytes 4718608 | tf_op jit(solution)/shard_map/all_gather | solution.py:69
  71.4 5.3 broadcast_in_dim.74
  76.7 162.8 %while.24 = (s32[]{:T(128)}, f32[64,64,576]{2,1,0:T(8,128)}, f32[2,64,576]{2,1,0:T(8,128)S(1)}, f32[32,512,128]{2,1,0:T(8,128)}, bf16[2,64,32,128]{3,2,1,0:T(8,1...) while((s32[]{:T(128)}, f32[64,64,576]{2,1,0:T(8,128)}, ...), condition=%wide.region_7.8_spmd.clone.clone, body=%wide.region_0.7_spmd.sunk.clone.clone.sunk | while | flops 14539294720 | bytes 202921360 | solution.py:94
  85.8 5.7 select_select_fusion.2
  101.0 5.3 fusion.92
  106.2 5.4 fusion.97
  111.7 5.3 fusion.98
  130.5 4.8 convert_bitcast_fusion.2
  141.2 4.7 copy_dynamic-update-slice_fusion.5
  145.9 5.0 select_add_fusion.2
  150.9 5.5 scatter_fusion
  165.5 5.7 select_select_fusion.2
  180.7 5.3 fusion.92
  186.0 5.4 fusion.97
  191.4 5.3 fusion.98
  210.2 4.8 convert_bitcast_fusion.2
  220.9 4.8 copy_dynamic-update-slice_fusion.5
  225.7 8.4 select_add_fusion.2
  234.1 5.4 scatter_fusion
  241.2 8.6 copy.29
  249.8 153.1 %all-reduce.1 = bf16[32,512,128]{2,1,0:T(8,128)(2,1)} all-reduce(f32[32,512,128]{2,1,0:T(8,128)} %get-tuple-element.223), channel_id=1, replica_groups=mesh['seq'=32,'head'=4] {'seq'}, use_global_device_ids=true, to_apply=%region_9.10 | all-reduce | flops 2097152 | bytes 12582912 | tf_op jit(solution)/shard_map/psum | solution.py:103
  402.9 486.4 %reduce-scatter.2.cloned.1.call-done = f32[32,576]{1,0:T(8,128)} async-done(((f32[4096,576]{1,0:T(8,128)}), f32[32,576]{1,0:T(8,128)}) %reduce-scatter.2.cloned.1.call-update) | async-done | bytes 73744 | tf_op jit(solution)/shard_map/reduce_scatter | solution.py:102
  (99 shorter events, 72.3 us)
Async XLA Ops:
  7.2 64.2 %all-gather.2.cloned.1.call-start = ((), (), s32[]{:S(2)}) async-start(), calls=%async_computation.1 | async-start | bytes 5406720 | tf_op jit(solution)/shard_map/all_gather | solution.py:69
  20.7 868.6 %reduce-scatter.2.cloned.1.call-start = ((), (), s32[]{:S(2)}) async-start(), calls=%async_computation.2 | async-start | bytes 10567680 | tf_op jit(solution)/shard_map/reduce_scatter | solution.py:102
  20.8 7.6 copy-start.6
  71.4 5.3 copy-start.5
  76.7 15.8 %copy-start.3 = (f32[2,64,576]{2,1,0:T(8,128)}, f32[2,64,576]{2,1,0:T(8,128)S(1)}, u32[]{:S(2)}) copy-start(f32[2,64,576]{2,1,0:T(8,128)S(1)} %get-tuple-element.572) | copy-start | bytes 884740 | tf_op jit(solution)/shard_map/while
  118.4 2.4 copy-start
  120.8 6.5 copy-start.1
  140.5 5.4 copy-start.2
  150.9 5.5 copy-start.4
  156.4 15.8 %copy-start.3 = (f32[2,64,576]{2,1,0:T(8,128)}, f32[2,64,576]{2,1,0:T(8,128)S(1)}, u32[]{:S(2)}) copy-start(f32[2,64,576]{2,1,0:T(8,128)S(1)} %get-tuple-element.572) | copy-start | bytes 884740 | tf_op jit(solution)/shard_map/while
  198.1 2.4 copy-start
  200.5 6.5 copy-start.1
  220.3 5.5 copy-start.2
  234.1 5.4 copy-start.4
Sparse Core Ops, SparseCore 0:
  20.8 50.5 all-gather.1
  241.3 647.8 reduce-scatter.1
where the time goes:
time: 905 us; the launch traced here: 896 us
  waiting for transfers between devices  529 us (58%)
  blocking collectives  166 us (18%)
  matrix products  73.3 us (8%)
  local copies, waits for them, and re-layouts  57.3 us (6%)
  other arithmetic  49.9 us (6%)
  between operations  14.1 us (2%)
    reduce_scatter x1, waiting for transfers between devices, on_device(): lax.psum_scatter(full_grad, ('seq', 'head'), scatter_dimension=0, tiled=T...  486 us
    psum x1, blocking collectives, on_device(): grad_uv = lax.psum(grad_weight, 'seq').astype(jnp.bfloat16)  153 us
    all_gather x1, waiting for transfers between devices, on_device(): whole = lax.all_gather(local_cache, 'seq', axis=0, tiled=True)  43 us
    gather x12, other arithmetic, key_mask(): return jnp.where(slot_pos == 0, col_pos <= row_pos, present[slot_pos])  19 us
  transfers between devices with their start and end apart: 2, of which 2 were waited for; matrix products, arithmetic and copies ran while one was open for 2% of the time, Pallas kernels for 0%

commit v1 on v0

v1 whole, which is shorter than its diff:
```python
import functools, jax, jax.numpy as jnp, numpy as np
from jax import lax
from jax.experimental import pallas as pl
from jax.experimental.pallas import tpu as pltpu
from jax.sharding import PartitionSpec as P

BLK=64; KEEP=15; SLOTS=16; KEYS=1024; DL=512; KV=576; KP=640; NH=32; VH=128; TD=128
ROWS=2048; TILE=256; NT=8
SC=192.0**-0.5
L2E=1.4426950408889634
NEG=-1e30
F32=jnp.float32; BF=jnp.bfloat16
NTD=(((1,),(1,)),((),()))
TND=(((0,),(0,)),((),()))

def halves(a,b):
    return (jnp.concatenate([a[:, :64], b[:, :64]],1), jnp.concatenate([a[:, 64:], b[:, 64:]],1))

def build_keys(g, lists_ref, full_ref, k_ref, kt_ref, own):
    colid = lax.broadcasted_iota(jnp.int32,(BLK,KP-DL),1)
    for j in range(SLOTS):
        if j==0:
            row = own+g; bias=jnp.float32(0.0)
        else:
            e = lists_ref[g, j-1]
            row = jnp.maximum(e,0)
            bias = jnp.where(e>=0, 0.0, NEG).astype(F32)
        blk = full_ref[row]
        k_ref[g, j*BLK:(j+1)*BLK, :DL] = blk[:, :DL]
        rot = jnp.concatenate([blk[:, DL:].astype(F32), jnp.zeros((BLK,64),F32)],1)
        rot = jnp.where(colid==64, bias, rot).astype(BF)
        k_ref[g, j*BLK:(j+1)*BLK, DL:] = rot
    for c in range(8):
        kt_ref[g, :, c*128:(c+1)*128] = jnp.swapaxes(k_ref[g, c*128:(c+1)*128, :], 0, 1)

def prep_q(qt_ref, qg_ref):
    def body(hp, _):
        a=qt_ref[2*hp]; b=qt_ref[2*hp+1]
        x,y=halves(a,b)
        col=pl.ds(pl.multiple_of(hp*128,128),128)
        qg_ref[0,:KV,col]=x
        qg_ref[1,:KV,col]=y
        return 0
    lax.fori_loop(0,16,body,0)
    r=lax.broadcasted_iota(jnp.int32,(64,ROWS),0)
    one=jnp.where(r==0,1.0,0.0).astype(BF)
    qg_ref[0,KV:,:]=one
    qg_ref[1,KV:,:]=one

def make_mask(mask_ref):
    r=lax.broadcasted_iota(jnp.int32,(BLK,TILE),0)
    c=lax.broadcasted_iota(jnp.int32,(BLK,TILE),1)
    mask_ref[...]=jnp.where(r<=(c%BLK),0.0,NEG).astype(F32)

def forward(qg,k,kt,w,gout,mask,pt,do,cen,ot,uv,ho):
    def tile(i,_):
        col=pl.ds(pl.multiple_of(i*TILE,TILE),TILE)
        for p in range(2):
            h=i*4+2*p
            d0=lax.dot_general(w[h],gout[h],NTD,preferred_element_type=F32).astype(BF)
            d1=lax.dot_general(w[h+1],gout[h+1],NTD,preferred_element_type=F32).astype(BF)
            x,y=halves(d0,d1)
            c2=pl.ds(pl.multiple_of(i*TILE+p*128,128),128)
            do[0,:,c2]=x
            do[1,:,c2]=y
        for g in range(2):
            s=jnp.dot(k[g],qg[g,:,col],preferred_element_type=F32)
            s=jnp.concatenate([s[:BLK]+mask[...],s[BLK:]],0)
            m=jnp.max(s,axis=0,keepdims=True)
            e=jnp.exp2((s-m)*(SC*L2E))
            l=jnp.sum(e,axis=0,keepdims=True)
            pb=e.astype(BF)
            pt[g,:,col]=pb
            inv=1.0/l
            o=jnp.dot(kt[g,:DL,:],pb,preferred_element_type=F32)*inv
            ot[g]=o.astype(BF)
            dn=(do[g,:,col].astype(F32)*inv).astype(BF)
            do[g,:,col]=dn
            cen[g,:,col]=jnp.broadcast_to(jnp.sum(o*dn.astype(F32),axis=0,keepdims=True),(8,TILE))
        for p in range(2):
            hh=halves(ot[0,:,p*128:(p+1)*128],ot[1,:,p*128:(p+1)*128])
            for q in range(2):
                h=i*4+2*p+q
                uv[h]=jnp.dot(hh[q],gout[h],preferred_element_type=F32).astype(BF)
                ho[h]=lax.dot_general(hh[q],w[h],TND,preferred_element_type=F32).astype(BF)
        return 0
    lax.fori_loop(0,NT,tile,0)

def back_ds(g,k,pt,do,cen,ds):
    def tile(i,_):
        col=pl.ds(pl.multiple_of(i*TILE,TILE),TILE)
        dp=jnp.dot(k[g,:,:DL],do[g,:,col],preferred_element_type=F32)
        x=pt[g,:,col].astype(F32)*(dp-cen[g,0:1,col])
        ds[g,:,col]=x.astype(BF)
        return 0
    lax.fori_loop(0,NT,tile,0)

def back_kv(g,qg,do,pt,ds,gk):
    def chunk(c,_):
        rows=pl.ds(pl.multiple_of(c*TILE,TILE),TILE)
        a=lax.dot_general(qg[g,:KV,:],ds[g,rows,:],NTD,preferred_element_type=F32)*SC
        b=lax.dot_general(do[g],pt[g,rows,:],NTD,preferred_element_type=F32)
        t=jnp.concatenate([a[:DL]+b,a[DL:],jnp.zeros((KP-KV,TILE),F32)],0)
        gk[g,rows,:]=jnp.swapaxes(t,0,1).astype(gk.dtype)
        return 0
    lax.fori_loop(0,KEYS//TILE,chunk,0)

def back_q(kt,ds,dq):
    def tile(i,_):
        col=pl.ds(pl.multiple_of(i*TILE,TILE),TILE)
        r=[ (jnp.dot(kt[g,:KV,:],ds[g,:,col],preferred_element_type=F32)*SC).astype(BF) for g in range(2)]
        for p in range(2):
            x,y=halves(r[0][:,p*128:(p+1)*128],r[1][:,p*128:(p+1)*128])
            dq[i*4+2*p]=x
            dq[i*4+2*p+1]=y
        return 0
    lax.fori_loop(0,NT,tile,0)

def kern(parts, own, lists, qt, full, w, gout, ho, dq, gk, uv, qg,k,kt,mask,pt,do,cen,ot,ds):
    own=own[0]
    if 'p' in parts:
        make_mask(mask); prep_q(qt,qg)
        for g in range(2): build_keys(g,lists,full,k,kt,own)
    if 'f' in parts: forward(qg,k,kt,w,gout,mask,pt,do,cen,ot,uv,ho)
    if 's' in parts:
        for g in range(2): back_ds(g,k,pt,do,cen,ds)
    if 'k' in parts:
        for g in range(2): back_kv(g,qg,do,pt,ds,gk)
    if 'q' in parts: back_q(kt,ds,dq)

def call(own,lists,qt,full,w,gout,parts='pfskq'):
    V=pl.BlockSpec(memory_space=pltpu.VMEM)
    S=pl.BlockSpec(memory_space=pltpu.SMEM)
    return pl.pallas_call(functools.partial(kern,parts),
      out_shape=(jax.ShapeDtypeStruct((NH,TD,VH),BF),jax.ShapeDtypeStruct((NH,KV,TD),BF),
                 jax.ShapeDtypeStruct((2,KEYS,KP),BF),jax.ShapeDtypeStruct((NH,DL,VH),BF)),
      in_specs=[S,S,V,V,V,V], out_specs=(V,V,V,V),
      scratch_shapes=[pltpu.VMEM((2,KP,ROWS),BF),pltpu.VMEM((2,KEYS,KP),BF),pltpu.VMEM((2,KP,KEYS),BF),
        pltpu.VMEM((BLK,TILE),F32),pltpu.VMEM((2,KEYS,ROWS),BF),pltpu.VMEM((2,DL,ROWS),BF),
        pltpu.VMEM((2,8,ROWS),F32),pltpu.VMEM((2,DL,TILE),BF),pltpu.VMEM((2,KEYS,ROWS),BF)],
      compiler_params=pltpu.CompilerParams(vmem_limit_bytes=62*2**20), name="latent_attn")(own,lists,qt,full,w,gout)
MESH = pl.DeviceIdType.MESH
NCH = 4
CROWS = NH * DL // NCH
CH = CROWS // 2
QA = CH // 4
QB = QA // 4


def place():
    s = lax.axis_index("seq")
    z = lax.axis_index("head")
    return s, z, s % 2, (s // 2) % 4, s // 8


def seq_at(y, x, c):
    return (y * 4 + x) * 2 + c


def rcopy(src, dst, ssem, rsem, s, z):
    return pltpu.make_async_remote_copy(
        src_ref=src, dst_ref=dst, send_sem=ssem, recv_sem=rsem, device_id=(s, z), device_id_type=MESH
    )


def greet(seq_steps, head_steps):
    s, z, _, _, _ = place()
    barrier = pltpu.get_barrier_semaphore()
    for d in seq_steps:
        pl.semaphore_signal(barrier, inc=1, device_id=((s + d) % 32, z), device_id_type=MESH)
    for d in head_steps:
        pl.semaphore_signal(barrier, inc=1, device_id=(s, (z + d) % 4), device_id_type=MESH)
    pl.semaphore_wait(barrier, len(seq_steps) + len(head_steps))


def gather_body(cache_ref, full, lsem, zs, zr, s1, r1, s2, r2, s3, r3, s4, r4, s5, r5):
    s, z, c, x, y = place()
    barrier = pltpu.get_barrier_semaphore()
    peers = [(s, (z + d) % 4) for d in (1, 2, 3)]
    for d in (1, 3):
        peers.append((seq_at(y, (x + d) % 4, c), z))
        peers.append((seq_at((y + d) % 4, x, c), z))
    peers.append((seq_at(y, x, 1 - c), z))
    for p in peers:
        pl.semaphore_signal(barrier, inc=1, device_id=p, device_id_type=MESH)
    pl.semaphore_wait(barrier, len(peers))

    def nbr_a(d):
        return seq_at((y + d * c) % 4, (x + d * (1 - c)) % 4, c)

    def nbr_b(d):
        return seq_at((y + d * (1 - c)) % 4, (x + d * c) % 4, c)

    def at(a, b):
        return full.at[(y + a * c + b * (1 - c)) % 4, (x + a * (1 - c) + b * c) % 4, c]

    def shard(a, b):
        return at(a, b)

    rows = pl.ds(pl.multiple_of(z * 32, 32), 32)
    own = at(0, 0)
    local = pltpu.make_async_copy(cache_ref, own.at[rows], lsem)
    local.start()
    pend = []
    zc = []
    for d in (1, 2, 3):
        q = rcopy(cache_ref, own.at[rows], zs.at[d - 1], zr.at[d - 1], s, (z + d) % 4)
        q.start()
        zc.append(q)
    local.wait()
    for q in zc:
        q.wait_recv()
    pend += zc

    def start(src, ssem, rsem, dev):
        q = rcopy(src, src, ssem, rsem, dev, z)
        q.start()
        pend.append(q)

    def got(dst, rsem):
        rcopy(dst, dst, s5.at[0], rsem, s, (z + 1) % 4).wait_recv()

    lo, hi = pl.ds(0, 64), pl.ds(64, 64)
    twin = seq_at(y, x, 1 - c)

    def to_twin(a, b):
        k = (a % 4) * 4 + b % 4
        start(shard(a, b), s5.at[k], r5.at[k], twin)

    def b_sends(a):
        k = a % 4
        start(shard(a, 0), s3.at[k, 0], r3.at[k, 0], nbr_b(1))
        start(shard(a, 0), s3.at[k, 1], r3.at[k, 1], nbr_b(-1))

    start(own, s1.at[0], r1.at[0], nbr_a(1))
    start(own, s1.at[1], r1.at[1], nbr_a(-1))
    b_sends(0)
    to_twin(0, 0)
    got(shard(-1, 0), r1.at[0])
    start(shard(-1, 0).at[lo], s2.at[0], r2.at[0], nbr_a(1))
    got(shard(1, 0), r1.at[1])
    start(shard(1, 0).at[hi], s2.at[1], r2.at[1], nbr_a(-1))
    b_sends(-1)
    b_sends(1)
    to_twin(-1, 0)
    to_twin(1, 0)

    def b_relay(a):
        k = a % 4
        got(shard(a, -1), r3.at[k, 0])
        start(shard(a, -1).at[lo], s4.at[k, 0], r4.at[k, 0], nbr_b(1))
        got(shard(a, 1), r3.at[k, 1])
        start(shard(a, 1).at[hi], s4.at[k, 1], r4.at[k, 1], nbr_b(-1))
        to_twin(a, -1)
        to_twin(a, 1)

    b_relay(0)
    got(shard(2, 0).at[lo], r2.at[0])
    got(shard(2, 0).at[hi], r2.at[1])
    b_sends(2)
    to_twin(2, 0)
    for a in (-1, 1, 2):
        b_relay(a)
    for a in (0, -1, 1, 2):
        k = a % 4
        got(shard(a, 2).at[lo], r4.at[k, 0])
        got(shard(a, 2).at[hi], r4.at[k, 1])
        to_twin(a, 2)
    for a in range(4):
        for b in range(4):
            dst = full.at[(y + a * (1 - c) + b * c) % 4, (x + a * c + b * (1 - c)) % 4, 1 - c]
            got(dst, r5.at[a * 4 + b])
    for q in pend:
        q.wait_send()


def gather(cache):
    sems = [pltpu.SemaphoreType.DMA]
    for shape in ((3,), (3,), (2,), (2,), (2,), (2,), (4, 2), (4, 2), (4, 2), (4, 2), (16,), (16,)):
        sems.append(pltpu.SemaphoreType.DMA(shape))
    return pl.pallas_call(
        gather_body,
        out_shape=jax.ShapeDtypeStruct((4, 4, 2, TD, KV), BF),
        in_specs=[pl.BlockSpec(memory_space=pltpu.VMEM)],
        out_specs=pl.BlockSpec(memory_space=pltpu.VMEM),
        scratch_shapes=sems,
        compiler_params=pltpu.CompilerParams(
            collective_id=0, has_side_effects=True, vmem_limit_bytes=60 * 2**20
        ),
        name="gather_cache",
    )(cache)


def uv_stages(u, o, rc, ra1, ra2, rb, rb1, rb2, ss, rs):
    s, z, c, x, y = place()
    twin = seq_at(y, x, 1 - c)
    pa = x * (1 - c) + y * c
    pb = y * (1 - c) + x * c

    def nbr_a(d):
        return seq_at((y + d * c) % 4, (x + d * (1 - c)) % 4, c)

    def nbr_b(d):
        return seq_at((y + d * (1 - c)) % 4, (x + d * c) % 4, c)

    def ds(start, size):
        return pl.ds(pl.multiple_of(start, size), size)

    def add(dst, dst_ix, terms):
        t = terms[0][...].astype(F32)
        for r in terms[1:]:
            t = t + r[...].astype(F32)
        dst[dst_ix] = t.astype(BF)

    def pair(k, st, a, b, nbr):
        return [
            rcopy(a[0], a[1], ss.at[k, st, 0], rs.at[k, st, 0], nbr(1), z),
            rcopy(b[0], b[1], ss.at[k, st, 1], rs.at[k, st, 1], nbr(-1), z),
        ]

    base = c * CH

    def out(k, start, size):
        return o.at[k, pl.ds(pl.multiple_of(start, size), size)]

    def c0(k):
        return [rcopy(u.at[k, ds((1 - c) * CH, CH)], rc.at[k], ss.at[k, 0, 0], rs.at[k, 0, 0], twin, z)]

    def c1(k):
        q = ((pa + 2) % 4) * QA
        return pair(k, 1, (rc.at[k, ds(q, QA // 2)], ra1.at[k, 0]),
                    (rc.at[k, ds(q + QA // 2, QA // 2)], ra1.at[k, 1]), nbr_a)

    def c2(k):
        return pair(k, 2, (rc.at[k, ds((pa + 1) % 4 * QA, QA)], ra2.at[k, 0]),
                    (rc.at[k, ds((pa + 3) % 4 * QA, QA)], ra2.at[k, 1]), nbr_a)

    def c3(k):
        q = ((pb + 2) % 4) * QB
        return pair(k, 3, (rb.at[k, ds(q, QB // 2)], rb1.at[k, 0]),
                    (rb.at[k, ds(q + QB // 2, QB // 2)], rb1.at[k, 1]), nbr_b)

    def c4(k):
        return pair(k, 4, (rb.at[k, ds((pb + 1) % 4 * QB, QB)], rb2.at[k, 0]),
                    (rb.at[k, ds((pb + 3) % 4 * QB, QB)], rb2.at[k, 1]), nbr_b)

    def c5(k):
        m = out(k, base + pa * QA + pb * QB, QB)
        return pair(k, 5, (m, m), (m, m), nbr_b)

    def c6(k):
        lo = out(k, base + pa * QA + (pb + 3) % 4 * QB, QB // 2)
        hi = out(k, base + pa * QA + (pb + 1) % 4 * QB + QB // 2, QB // 2)
        return pair(k, 6, (lo, lo), (hi, hi), nbr_b)

    def c7(k):
        m = out(k, base + pa * QA, QA)
        return pair(k, 7, (m, m), (m, m), nbr_a)

    def c8(k):
        lo = out(k, base + (pa + 3) % 4 * QA, QA // 2)
        hi = out(k, base + (pa + 1) % 4 * QA + QA // 2, QA // 2)
        return pair(k, 8, (lo, lo), (hi, hi), nbr_a)

    def c9(k):
        m = out(k, base, CH)
        return [rcopy(m, m, ss.at[k, 9, 0], rs.at[k, 9, 0], twin, z)]

    def got5(k):
        return [out(k, base + pa * QA + (pb + 3) % 4 * QB, QB), out(k, base + pa * QA + (pb + 1) % 4 * QB, QB)]

    def got6(k):
        q = base + pa * QA + (pb + 2) % 4 * QB
        return [out(k, q, QB // 2), out(k, q + QB // 2, QB // 2)]

    def got7(k):
        return [out(k, base + (pa + 3) % 4 * QA, QA), out(k, base + (pa + 1) % 4 * QA, QA)]

    def got8(k):
        q = base + (pa + 2) % 4 * QA
        return [out(k, q, QA // 2), out(k, q + QA // 2, QA // 2)]

    def got9(k):
        return [out(k, (1 - c) * CH, CH)]

    makers = [c0, c1, c2, c3, c4, c5, c6, c7, c8, c9]

    def arrived(k, st):
        if st in (0, 1, 2, 3, 4):
            for q in makers[st](k):
                q.wait_recv()
        else:
            for i, dst in enumerate({5: got5, 6: got6, 7: got7, 8: got8, 9: got9}[st](k)):
                rcopy(dst, dst, ss.at[k, st, i], rs.at[k, st, i], twin, z).wait_recv()
        for q in makers[st](k):
            q.wait_send()

    def stage(k, st):
        if st > 0:
            arrived(k, st - 1)
        if st == 1:
            add(rc, (k,), [u.at[k, ds(base, CH)], rc.at[k]])
        elif st == 2:
            a = ds((pa + 1) % 4 * QA, QA // 2)
            b = ds((pa + 3) % 4 * QA + QA // 2, QA // 2)
            add(rc, (k, a), [rc.at[k, a], ra1.at[k, 0]])
            add(rc, (k, b), [rc.at[k, b], ra1.at[k, 1]])
        elif st == 3:
            add(rb, (k,), [rc.at[k, ds(pa * QA, QA)], ra2.at[k, 0], ra2.at[k, 1]])
        elif st == 4:
            a = ds((pb + 1) % 4 * QB, QB // 2)
            b = ds((pb + 3) % 4 * QB + QB // 2, QB // 2)
            add(rb, (k, a), [rb.at[k, a], rb1.at[k, 0]])
            add(rb, (k, b), [rb.at[k, b], rb1.at[k, 1]])
        elif st == 5:
            add(o, (k, ds(base + pa * QA + pb * QB, QB)),
                [rb.at[k, ds(pb * QB, QB)], rb2.at[k, 0], rb2.at[k, 1]])
        if st < 10:
            for q in makers[st](k):
                q.start()

    return stage


UV_SCRATCH = [
    pltpu.VMEM((NCH, CH, 128), BF),
    pltpu.VMEM((NCH, 2, QA // 2, 128), BF),
    pltpu.VMEM((NCH, 2, QA, 128), BF),
    pltpu.VMEM((NCH, QA, 128), BF),
    pltpu.VMEM((NCH, 2, QB // 2, 128), BF),
    pltpu.VMEM((NCH, 2, QB, 128), BF),
    pltpu.SemaphoreType.DMA((NCH, 10, 2)),
    pltpu.SemaphoreType.DMA((NCH, 10, 2)),
]


def cache_stages(inv, flag, gk, gc, zr1, zr2, rz, send, recv, part, zss, zrs, xss, xrs, fss, frs):
    s, z, c, x, y = place()
    z1, z2, z3 = (z + 1) % 4, (z + 2) % 4, (z + 3) % 4

    def first(g):
        return [
            rcopy(gk.at[g, 0:8, z2], zr1.at[g, 0], zss.at[g, 0, 0], zrs.at[g, 0, 0], s, z1),
            rcopy(gk.at[g, 8:16, z2], zr1.at[g, 1], zss.at[g, 0, 1], zrs.at[g, 0, 1], s, z3),
        ]

    def second(g):
        return [
            rcopy(gk.at[g, :, z1], zr2.at[g, 0], zss.at[g, 1, 0], zrs.at[g, 1, 0], s, z1),
            rcopy(gk.at[g, :, z3], zr2.at[g, 1], zss.at[g, 1, 1], zrs.at[g, 1, 1], s, z3),
        ]

    def head_send(g):
        for q in first(g):
            q.start()

    def head_relay(g):
        for q in first(g):
            q.wait()
        gk[g, 0:8, z1] = (gk[g, 0:8, z1].astype(F32) + zr1[g, 0].astype(F32)).astype(BF)
        gk[g, 8:16, z3] = (gk[g, 8:16, z3].astype(F32) + zr1[g, 1].astype(F32)).astype(BF)
        for q in second(g):
            q.start()

    def head_sum(g):
        for q in second(g):
            q.wait()
        rz[g, 0:16] = (gk[g, :, z].astype(F32) + zr2[g, 0].astype(F32) + zr2[g, 1].astype(F32)).astype(BF)
        rz[g, 16] = jnp.zeros((16, KP), BF)

    col = lax.broadcasted_iota(jnp.int32, (16, KP), 1)

    def spread():
        for d in range(32):
            t = (s + d) % 32
            v = rz[0, inv[0, t]].astype(F32) + rz[1, inv[1, t]].astype(F32)
            v = jnp.where(col == KV, flag[t], v)
            send[d] = v.astype(BF)
            if d:
                rcopy(send.at[d], recv.at[d], xss.at[d], xrs.at[d], t, z).start()

    def collect():
        a = jnp.zeros((16, KP), F32)
        b = jnp.zeros((16, KP), F32)
        for d in range(32):
            if d:
                q = rcopy(send.at[d], recv.at[d], xss.at[d], xrs.at[d], (s + d) % 32, z)
                q.wait()
                v = recv[d].astype(F32)
            else:
                v = send[0].astype(F32)
            f = v[:, KV : KV + 1]
            second_part = v * f
            b = b + second_part
            a = a + (v - second_part)
        part[0, 0] = a + rz[0, 0].astype(F32)
        part[0, 1] = b + rz[1, 0].astype(F32)
        for d in (1, 2, 3):
            rcopy(part.at[0], part.at[d], fss.at[d - 1], frs.at[d - 1], s, (z + d) % 4).start()

    def finish():
        for d in (1, 2, 3):
            rcopy(part.at[0], part.at[d], fss.at[d - 1], frs.at[d - 1], s, (z + d) % 4).wait()
        q = 2 * (z % 2)
        gc[0:16] = part[(z - q + 4) % 4, z // 2][:, :KV]
        gc[16:32] = part[(z - q + 3) % 4, z // 2][:, :KV]

    return head_send, head_relay, head_sum, spread, collect, finish


CACHE_SCRATCH = [
    pltpu.VMEM((2, 2, 8, 16, KP), BF),
    pltpu.VMEM((2, 2, 16, 16, KP), BF),
    pltpu.VMEM((2, 17, 16, KP), BF),
    pltpu.VMEM((32, 16, KP), BF),
    pltpu.VMEM((32, 16, KP), BF),
    pltpu.VMEM((4, 2, 16, KP), F32),
    pltpu.SemaphoreType.DMA((2, 2, 2)),
    pltpu.SemaphoreType.DMA((2, 2, 2)),
    pltpu.SemaphoreType.DMA((32,)),
    pltpu.SemaphoreType.DMA((32,)),
    pltpu.SemaphoreType.DMA((3,)),
    pltpu.SemaphoreType.DMA((3,)),
]


def reduce_body(inv, flag, u, gk_in, o, gc, gk, *scr):
    uv_scr, cache_scr = scr[: len(UV_SCRATCH)], scr[len(UV_SCRATCH) :]
    greet(range(1, 32), (1, 2, 3))
    stage = uv_stages(u, o, *uv_scr)
    head_send, head_relay, head_sum, spread, collect, finish = cache_stages(inv, flag, gk, gc, *cache_scr)
    gk[...] = gk_in[...]
    for g in range(2):
        head_send(g)
    steps = {3: [lambda: head_relay(0)], 4: [lambda: head_relay(1)], 6: [lambda: head_sum(0)],
             7: [lambda: head_sum(1), spread], 9: [collect], 10: [finish]}
    for slot in range(NCH + 10):
        for st in range(11):
            k = slot - st
            if 0 <= k < NCH:
                stage(k, st)
        for f in steps.get(slot, []):
            f()


def reduce(inv, flag, u, gk):
    v = pl.BlockSpec(memory_space=pltpu.VMEM)
    m = pl.BlockSpec(memory_space=pltpu.SMEM)
    return pl.pallas_call(
        reduce_body,
        out_shape=(jax.ShapeDtypeStruct((NCH, CROWS, 128), BF), jax.ShapeDtypeStruct((32, KV), F32)),
        in_specs=[m, m, v, v],
        out_specs=(v, v),
        scratch_shapes=[pltpu.VMEM((2, 16, 4, 16, KP), BF)] + UV_SCRATCH + CACHE_SCRATCH,
        compiler_params=pltpu.CompilerParams(
            collective_id=1, has_side_effects=True, vmem_limit_bytes=60 * 2**20
        ),
        name="reduce_grads",
    )(inv, flag, u, gk)


def on_device(queries, cache, lists, w_uv, grad_out):
    first_block = lax.axis_index("seq") * 2
    full = gather(cache).reshape(64, BLK, KV)
    ho, dq, gk, uv = call(first_block.reshape(1), lists, queries.transpose(1, 2, 0), full, w_uv, grad_out.transpose(1, 0, 2))
    shard = jnp.where(lists >= 0, lists // 2, -1)
    hit = shard[:, None, :] == jnp.arange(32)[None, :, None]
    inv = jnp.min(jnp.where(hit, jnp.arange(1, 16), 16), axis=-1).astype(jnp.int32)
    flag = jnp.max(jnp.where(hit, (lists % 2)[:, None, :], 0), axis=(0, 2)).astype(F32)
    o, gc = reduce(inv, flag, uv.reshape(NCH, CROWS, 128), gk.reshape(2, 16, 4, 16, KP))
    return ho.transpose(1, 0, 2), dq.transpose(2, 0, 1), gc, o.reshape(NH, DL, VH)


def solution(mesh):
    return jax.shard_map(
        on_device,
        mesh=mesh,
        in_specs=(
            P("seq", "head", None),
            P(("seq", "head"), None),
            P("seq", None),
            P("head", None, None),
            P("seq", "head", None),
        ),
        out_specs=(
            P("seq", "head", None),
            P("seq", "head", None),
            P(("seq", "head"), None),
            P("head", None, None),
        ),
        check_vma=False,
    )
```

time: 905 us -> 184 us (0.20)
  waiting for transfers between devices: 529 us -> 0 us
  Pallas kernels: 0 us -> 173 us
  blocking collectives: 166 us -> 0 us
  matrix products: 73.3 us -> 0 us
  other arithmetic: 49.9 us -> 1.21 us
  local copies, waits for them, and re-layouts: 57.3 us -> 9.41 us
  between operations: 14.1 us -> 0.69 us
    reduce_scatter x1 -> x0, waiting for transfers between devices: 486 us -> none  [on_device(): lax.psum_scatter(full_grad, ('seq', 'head'), scatter_dimension=0, tiled=T...]
    pallas_call x0 -> x3, Pallas kernels: none -> 173 us  [the longest x1 75.1 us: call(): pl.pallas_call(functools.partial(kern, parts), out_shape=(jax.ShapeDtypeS...]
    psum x1 -> x0, blocking collectives: 153 us -> none  [on_device(): grad_uv = lax.psum(grad_weight, 'seq').astype(jnp.bfloat16)]
    dot_general x18 -> x0, matrix products: 73.3 us -> none  [the longest x2 13.4 us: block_pass(): jnp.einsum('rhd,rhe->hde', latent_out, grad_rows, preferred_element_type=...]
    all_gather x1 -> x0, waiting for transfers between devices: 43 us -> none  [on_device(): whole = lax.all_gather(local_cache, 'seq', axis=0, tiled=True)]
    gather x14 -> x0, other arithmetic: 19 us -> none  [the longest x12 19 us: key_mask(): return jnp.where(slot_pos == 0, col_pos <= row_pos, present[slot_pos])]
    all_gather x1 -> x0, blocking collectives: 13.4 us -> none  [on_device(): local_cache = lax.all_gather(cache, 'head', axis=0, tiled=True)]
    dynamic_update_slice x4 -> x0, local copies, waits for them, and re-layouts: 11.8 us -> none  [on_device(): lax.scan(step, init, jnp.arange(per_dev, dtype=jnp.int32))]
  transfers between devices with their start and end apart: 2 -> 0, of which waited for: 2 -> 0; matrix products, arithmetic and copies ran while one was open for 2% -> 0% of each run, Pallas kernels for 0% -> 0%
where the time goes in v1:
time: 184 us
  Pallas kernels  173 us (94%)
  local copies, waits for them, and re-layouts  9.41 us (5%)
    pallas_call x1, Pallas kernels, call(): pl.pallas_call(functools.partial(kern, parts), out_shape=(jax.ShapeDtypeS...  75.1 us
    pallas_call x1, Pallas kernels, reduce(): pl.pallas_call(reduce_body, out_shape=(jax.ShapeDtypeStruct((NCH, CROWS,...  63.3 us
    pallas_call x1, Pallas kernels, gather(): pl.pallas_call(gather_body, out_shape=jax.ShapeDtypeStruct((4, 4, 2, TD,...  34.2 us
    unnamed x10, local copies, waits for them, and re-layouts  9.22 us

profile of v1, /device:TPU:1, one launch (start us, length us, event | category | flops | bytes accessed | tf_op | source)
XLA Modules:
  0.0 183.9 jit_solution(7773918876301223878)
XLA Ops:
  0.6 0.0 copy-start
  0.6 34.2 %gather_cache.1 = bf16[4,4,2,128,576]{4,3,2,1,0:T(8,128)(2,1)} custom-call(bf16[32,576]{1,0:T(8,128)(2,1)} %cache_ref.1), custom_call_target="tpu_custom_call" | custom-call | tf_op jit(solution)/shard_map/gather_cache/pallas_call | solution.py:281
  34.9 0.0 copy-done
  34.9 1.4 copy.16
  36.3 0.0 copy-start.2
  36.3 75.1 %latent_attn.1 = (bf16[32,128,128]{2,1,0:T(8,128)(2,1)}, bf16[32,576,128]{2,1,0:T(8,128)(2,1)}, bf16[2,1024,640]{2,1,0:T(8,128)(2,1)}, bf16[32,512,128]{2,1,0:T(8,128)(2,1)}) custom-call(s32[1]{0:T(128)} %bitcast.own, s32[2,15]{1,0:T(2,128)} %lists.1, bf16[32,576,128]{2,1,0:T(8,128)(2,1)} %bitcast.12, bf16[64,64,576]{2,1,0:T(8,128)(2,1)} %bitcast.11, ...), custom_call_target="tpu_custom_call" | custom-call | tf_op jit(solution)/shard_map/latent_attn/pallas_call | solution.py:134
  111.3 0.0 copy-start.1
  111.3 0.0 copy-done.2
  111.3 0.1 copy.12
  111.4 0.1 copy.13
  111.5 0.7 select_reduce_fusion
  112.2 0.5 convert_element_type.3.flag
  112.7 63.3 %reduce_grads.1 = (bf16[4,4096,128]{2,1,0:T(8,128)(2,1)}, f32[32,576]{1,0:T(8,128)}) custom-call(s32[2,32]{1,0:T(2,128)} %get-tuple-element.25.inv, f32[32]{0:T(128)} %convert_element_type.3.flag, bf16[4,4096,128]{2,1,0:T(8,128)(2,1)} %bitcast.13, bf16[2,16,4,16,640]{4,3,2,1,0:T(8,128)(2,1)} %bitcast.16), custom_call_target="tpu_custom_call" | custom-call | tf_op jit(solution)/shard_map/reduce_grads/pallas_call | solution.py:549
  176.1 0.0 copy-done.1
  176.1 1.6 copy.14
  177.7 1.5 copy.19
  179.3 4.7 %copy.20 = bf16[32,512,128]{2,1,0:T(8,128)(2,1)} copy(bf16[32,512,128]{2,1,0:T(8,128)(2,1)} %bitcast.15) | data formatting | bytes 8388608
  (2 shorter events, 0.0 us)
Async XLA Ops:
  0.6 34.2 %copy-start = (bf16[128,32,128]{2,1,0:T(8,128)(2,1)S(1)}, bf16[128,32,128]{2,1,0:T(8,128)(2,1)}, u32[]{:S(2)}) copy-start(bf16[128,32,128]{2,1,0:T(8,128)(2,1)} %param.9) | copy-start | bytes 3145732
  36.3 75.1 %copy-start.2 = (s32[2,15]{1,0:T(2,128)S(1)}, s32[2,15]{1,0:T(2,128)}, u32[]{:S(2)}) copy-start(s32[2,15]{1,0:T(2,128)} %lists.1) | copy-start | bytes 364
  111.3 64.8 %copy-start.1 = (bf16[32,128,128]{2,1,0:T(8,128)(2,1)S(1)}, bf16[32,128,128]{2,1,0:T(8,128)(2,1)}, u32[]{:S(2)}) copy-start(bf16[32,128,128]{2,1,0:T(8,128)(2,1)} %get-tuple-element.10) | copy-start | bytes 3145732

commit v2 on v1

v2 whole, which is shorter than its diff:
```python
import functools, jax, jax.numpy as jnp, numpy as np
from jax import lax
from jax.experimental import pallas as pl
from jax.experimental.pallas import tpu as pltpu
from jax.sharding import PartitionSpec as P

BLK=64; KEEP=15; SLOTS=16; KEYS=1024; DL=512; KV=576; KP=640; NH=32; VH=128; TD=128
ROWS=2048; TILE=256; NT=8
SC=192.0**-0.5
L2E=1.4426950408889634
NEG=-1e30
F32=jnp.float32; BF=jnp.bfloat16
NTD=(((1,),(1,)),((),()))
TND=(((0,),(0,)),((),()))

def halves(a,b):
    return (jnp.concatenate([a[:, :64], b[:, :64]],1), jnp.concatenate([a[:, 64:], b[:, 64:]],1))

def make_mask(mask_ref):
    r=lax.broadcasted_iota(jnp.int32,(BLK,TILE),0)
    c=lax.broadcasted_iota(jnp.int32,(BLK,TILE),1)
    mask_ref[...]=jnp.where(r<=(c%BLK),0.0,NEG).astype(F32)

MESH = pl.DeviceIdType.MESH
NCH = 4
CROWS = NH * DL // NCH
CH = CROWS // 2
QA = CH // 4
QB = QA // 4


def place():
    s = lax.axis_index("seq")
    z = lax.axis_index("head")
    return s, z, s % 2, (s // 2) % 4, s // 8


def seq_at(y, x, c):
    return (y * 4 + x) * 2 + c


def rcopy(src, dst, ssem, rsem, s, z):
    return pltpu.make_async_remote_copy(
        src_ref=src, dst_ref=dst, send_sem=ssem, recv_sem=rsem, device_id=(s, z), device_id_type=MESH
    )


def greet(seq_steps, head_steps):
    s, z, _, _, _ = place()
    barrier = pltpu.get_barrier_semaphore()
    for d in seq_steps:
        pl.semaphore_signal(barrier, inc=1, device_id=((s + d) % 32, z), device_id_type=MESH)
    for d in head_steps:
        pl.semaphore_signal(barrier, inc=1, device_id=(s, (z + d) % 4), device_id_type=MESH)
    pl.semaphore_wait(barrier, len(seq_steps) + len(head_steps))


def uv_stages(u, o, rc, ra1, ra2, rb, rb1, rb2, ss, rs):
    s, z, c, x, y = place()
    twin = seq_at(y, x, 1 - c)
    pa = x * (1 - c) + y * c
    pb = y * (1 - c) + x * c

    def nbr_a(d):
        return seq_at((y + d * c) % 4, (x + d * (1 - c)) % 4, c)

    def nbr_b(d):
        return seq_at((y + d * (1 - c)) % 4, (x + d * c) % 4, c)

    def ds(start, size):
        return pl.ds(pl.multiple_of(start, size), size)

    def add(dst, dst_ix, terms):
        t = terms[0][...].astype(F32)
        for r in terms[1:]:
            t = t + r[...].astype(F32)
        dst[dst_ix] = t.astype(BF)

    def pair(k, st, a, b, nbr):
        return [
            rcopy(a[0], a[1], ss.at[k, st, 0], rs.at[k, st, 0], nbr(1), z),
            rcopy(b[0], b[1], ss.at[k, st, 1], rs.at[k, st, 1], nbr(-1), z),
        ]

    base = c * CH

    def out(k, start, size):
        return o.at[k, pl.ds(pl.multiple_of(start, size), size)]

    def c0(k):
        return [rcopy(u.at[k, ds((1 - c) * CH, CH)], rc.at[k], ss.at[k, 0, 0], rs.at[k, 0, 0], twin, z)]

    def c1(k):
        q = ((pa + 2) % 4) * QA
        return pair(k, 1, (rc.at[k, ds(q, QA // 2)], ra1.at[k, 0]),
                    (rc.at[k, ds(q + QA // 2, QA // 2)], ra1.at[k, 1]), nbr_a)

    def c2(k):
        return pair(k, 2, (rc.at[k, ds((pa + 1) % 4 * QA, QA)], ra2.at[k, 0]),
                    (rc.at[k, ds((pa + 3) % 4 * QA, QA)], ra2.at[k, 1]), nbr_a)

    def c3(k):
        q = ((pb + 2) % 4) * QB
        return pair(k, 3, (rb.at[k, ds(q, QB // 2)], rb1.at[k, 0]),
                    (rb.at[k, ds(q + QB // 2, QB // 2)], rb1.at[k, 1]), nbr_b)

    def c4(k):
        return pair(k, 4, (rb.at[k, ds((pb + 1) % 4 * QB, QB)], rb2.at[k, 0]),
                    (rb.at[k, ds((pb + 3) % 4 * QB, QB)], rb2.at[k, 1]), nbr_b)

    def c5(k):
        m = out(k, base + pa * QA + pb * QB, QB)
        return pair(k, 5, (m, m), (m, m), nbr_b)

    def c6(k):
        lo = out(k, base + pa * QA + (pb + 3) % 4 * QB, QB // 2)
        hi = out(k, base + pa * QA + (pb + 1) % 4 * QB + QB // 2, QB // 2)
        return pair(k, 6, (lo, lo), (hi, hi), nbr_b)

    def c7(k):
        m = out(k, base + pa * QA, QA)
        return pair(k, 7, (m, m), (m, m), nbr_a)

    def c8(k):
        lo = out(k, base + (pa + 3) % 4 * QA, QA // 2)
        hi = out(k, base + (pa + 1) % 4 * QA + QA // 2, QA // 2)
        return pair(k, 8, (lo, lo), (hi, hi), nbr_a)

    def c9(k):
        m = out(k, base, CH)
        return [rcopy(m, m, ss.at[k, 9, 0], rs.at[k, 9, 0], twin, z)]

    def got5(k):
        return [out(k, base + pa * QA + (pb + 3) % 4 * QB, QB), out(k, base + pa * QA + (pb + 1) % 4 * QB, QB)]

    def got6(k):
        q = base + pa * QA + (pb + 2) % 4 * QB
        return [out(k, q, QB // 2), out(k, q + QB // 2, QB // 2)]

    def got7(k):
        return [out(k, base + (pa + 3) % 4 * QA, QA), out(k, base + (pa + 1) % 4 * QA, QA)]

    def got8(k):
        q = base + (pa + 2) % 4 * QA
        return [out(k, q, QA // 2), out(k, q + QA // 2, QA // 2)]

    def got9(k):
        return [out(k, (1 - c) * CH, CH)]

    makers = [c0, c1, c2, c3, c4, c5, c6, c7, c8, c9]

    def arrived(k, st):
        if st in (0, 1, 2, 3, 4):
            for q in makers[st](k):
                q.wait_recv()
        else:
            for i, dst in enumerate({5: got5, 6: got6, 7: got7, 8: got8, 9: got9}[st](k)):
                rcopy(dst, dst, ss.at[k, st, i], rs.at[k, st, i], twin, z).wait_recv()
        for q in makers[st](k):
            q.wait_send()

    def stage(k, st):
        if st > 0:
            arrived(k, st - 1)
        if st == 1:
            add(rc, (k,), [u.at[k, ds(base, CH)], rc.at[k]])
        elif st == 2:
            a = ds((pa + 1) % 4 * QA, QA // 2)
            b = ds((pa + 3) % 4 * QA + QA // 2, QA // 2)
            add(rc, (k, a), [rc.at[k, a], ra1.at[k, 0]])
            add(rc, (k, b), [rc.at[k, b], ra1.at[k, 1]])
        elif st == 3:
            add(rb, (k,), [rc.at[k, ds(pa * QA, QA)], ra2.at[k, 0], ra2.at[k, 1]])
        elif st == 4:
            a = ds((pb + 1) % 4 * QB, QB // 2)
            b = ds((pb + 3) % 4 * QB + QB // 2, QB // 2)
            add(rb, (k, a), [rb.at[k, a], rb1.at[k, 0]])
            add(rb, (k, b), [rb.at[k, b], rb1.at[k, 1]])
        elif st == 5:
            add(o, (k, ds(base + pa * QA + pb * QB, QB)),
                [rb.at[k, ds(pb * QB, QB)], rb2.at[k, 0], rb2.at[k, 1]])
        if st < 10:
            for q in makers[st](k):
                q.start()

    return stage


UV_SCRATCH = [
    pltpu.VMEM((NCH, CH, 128), BF),
    pltpu.VMEM((NCH, 2, QA // 2, 128), BF),
    pltpu.VMEM((NCH, 2, QA, 128), BF),
    pltpu.VMEM((NCH, QA, 128), BF),
    pltpu.VMEM((NCH, 2, QB // 2, 128), BF),
    pltpu.VMEM((NCH, 2, QB, 128), BF),
    pltpu.SemaphoreType.DMA((NCH, 10, 2)),
    pltpu.SemaphoreType.DMA((NCH, 10, 2)),
]


class Gather:
    def __init__(self, cache_ref, full, lsem, zs, zr, s1, r1, s2, r2, s3, r3, s4, r4, s5, r5):
        self.__dict__.update(locals())
        self.pend = []

    def at(self, a, b, part=None):
        _, _, c, x, y = place()
        t = seq_at((y + a * c + b * (1 - c)) % 4, (x + a * (1 - c) + b * c) % 4, c)
        return self.block(t, part)

    def block(self, t, part):
        if part is None:
            return self.full.at[pl.ds(2 * t, 2)]
        return self.full.at[2 * t + part]

    def nbr_a(self, d):
        _, _, c, x, y = place()
        return seq_at((y + d * c) % 4, (x + d * (1 - c)) % 4, c)

    def nbr_b(self, d):
        _, _, c, x, y = place()
        return seq_at((y + d * (1 - c)) % 4, (x + d * c) % 4, c)

    def start(self, src, ssem, rsem, dev):
        q = rcopy(src, src, ssem, rsem, dev, place()[1])
        q.start()
        self.pend.append(q)

    def got(self, dst, rsem):
        s, z, _, _, _ = place()
        rcopy(dst, dst, self.s5.at[0], rsem, s, (z + 1) % 4).wait_recv()

    def to_twin(self, a, b):
        _, _, c, x, y = place()
        k = (a % 4) * 4 + b % 4
        self.start(self.at(a, b), self.s5.at[k], self.r5.at[k], seq_at(y, x, 1 - c))

    def b_sends(self, a):
        k = a % 4
        self.start(self.at(a, 0), self.s3.at[k, 0], self.r3.at[k, 0], self.nbr_b(1))
        self.start(self.at(a, 0), self.s3.at[k, 1], self.r3.at[k, 1], self.nbr_b(-1))

    def b_relay(self, a):
        k = a % 4
        self.got(self.at(a, -1), self.r3.at[k, 0])
        self.start(self.at(a, -1, 0), self.s4.at[k, 0], self.r4.at[k, 0], self.nbr_b(1))
        self.got(self.at(a, 1), self.r3.at[k, 1])
        self.start(self.at(a, 1, 1), self.s4.at[k, 1], self.r4.at[k, 1], self.nbr_b(-1))
        self.to_twin(a, -1)
        self.to_twin(a, 1)

    def step0(self):
        s, z, _, _, _ = place()
        mine = self.full.at[2 * s + z // 2, pl.ds(pl.multiple_of((z % 2) * 32, 32), 32)]
        self.local = pltpu.make_async_copy(self.cache_ref, mine, self.lsem)
        self.local.start()
        self.zc = [
            rcopy(self.cache_ref, mine, self.zs.at[d - 1], self.zr.at[d - 1], s, (z + d) % 4) for d in (1, 2, 3)
        ]
        for q in self.zc:
            q.start()
        self.pend += self.zc

    def step1(self):
        self.local.wait()
        for q in self.zc:
            q.wait_recv()
        self.start(self.at(0, 0), self.s1.at[0], self.r1.at[0], self.nbr_a(1))
        self.start(self.at(0, 0), self.s1.at[1], self.r1.at[1], self.nbr_a(-1))
        self.b_sends(0)
        self.to_twin(0, 0)

    def step2(self):
        self.got(self.at(-1, 0), self.r1.at[0])
        self.start(self.at(-1, 0, 0), self.s2.at[0], self.r2.at[0], self.nbr_a(1))
        self.got(self.at(1, 0), self.r1.at[1])
        self.start(self.at(1, 0, 1), self.s2.at[1], self.r2.at[1], self.nbr_a(-1))
        self.b_sends(-1)
        self.b_sends(1)
        self.to_twin(-1, 0)
        self.to_twin(1, 0)

    def step3(self):
        self.b_relay(0)
        self.got(self.at(2, 0, 0), self.r2.at[0])
        self.got(self.at(2, 0, 1), self.r2.at[1])
        self.b_sends(2)
        self.to_twin(2, 0)

    def step4(self):
        for a in (-1, 1):
            self.b_relay(a)

    def step5(self):
        self.b_relay(2)

    def step6(self):
        for a in (0, -1, 1, 2):
            k = a % 4
            self.got(self.at(a, 2, 0), self.r4.at[k, 0])
            self.got(self.at(a, 2, 1), self.r4.at[k, 1])
            self.to_twin(a, 2)

    def step7(self):
        _, _, c, x, y = place()
        for a in range(4):
            for b in range(4):
                t = seq_at((y + a * (1 - c) + b * c) % 4, (x + a * c + b * (1 - c)) % 4, 1 - c)
                self.got(self.block(t, None), self.r5.at[a * 4 + b])
        for q in self.pend:
            q.wait_send()


GATHER_SCRATCH = [pltpu.VMEM((64, BLK, KV), BF), pltpu.SemaphoreType.DMA] + [
    pltpu.SemaphoreType.DMA(shape)
    for shape in ((3,), (3,), (2,), (2,), (2,), (2,), (4, 2), (4, 2), (4, 2), (4, 2), (16,), (16,))
]


def cache_stages(inv, flag, gk, gc, zr1, zr2, rz, send, recv, part, zss, zrs, xss, xrs, fss, frs):
    s, z, c, x, y = place()
    z1, z2, z3 = (z + 1) % 4, (z + 2) % 4, (z + 3) % 4

    def first(u):
        g, b = u // 2, u % 2 * 8
        return [
            rcopy(gk.at[g, b : b + 4, z2], zr1.at[u, 0], zss.at[u, 0, 0], zrs.at[u, 0, 0], s, z1),
            rcopy(gk.at[g, b + 4 : b + 8, z2], zr1.at[u, 1], zss.at[u, 0, 1], zrs.at[u, 0, 1], s, z3),
        ]

    def second(u):
        g, b = u // 2, u % 2 * 8
        return [
            rcopy(gk.at[g, b : b + 8, z1], zr2.at[u, 0], zss.at[u, 1, 0], zrs.at[u, 1, 0], s, z1),
            rcopy(gk.at[g, b : b + 8, z3], zr2.at[u, 1], zss.at[u, 1, 1], zrs.at[u, 1, 1], s, z3),
        ]

    def head_send(u):
        for q in first(u):
            q.start()

    def head_relay(u):
        g, b = u // 2, u % 2 * 8
        for q in first(u):
            q.wait()
        gk[g, b : b + 4, z1] = (gk[g, b : b + 4, z1].astype(F32) + zr1[u, 0].astype(F32)).astype(BF)
        gk[g, b + 4 : b + 8, z3] = (gk[g, b + 4 : b + 8, z3].astype(F32) + zr1[u, 1].astype(F32)).astype(BF)
        for q in second(u):
            q.start()

    def head_sum(u):
        g, b = u // 2, u % 2 * 8
        for q in second(u):
            q.wait()
        t = gk[g, b : b + 8, z].astype(F32) + zr2[u, 0].astype(F32) + zr2[u, 1].astype(F32)
        rz[g, b : b + 8] = t.astype(BF)
        if b:
            rz[g, 16] = jnp.zeros((16, KP), BF)

    col = lax.broadcasted_iota(jnp.int32, (16, KP), 1)

    def spread():
        for d in range(32):
            t = (s + d) % 32
            v = rz[0, inv[0, t]].astype(F32) + rz[1, inv[1, t]].astype(F32)
            v = jnp.where(col == KV, flag[t], v)
            send[d] = v.astype(BF)
            if d:
                rcopy(send.at[d], recv.at[d], xss.at[d], xrs.at[d], t, z).start()

    def collect():
        a = jnp.zeros((16, KP), F32)
        b = jnp.zeros((16, KP), F32)
        for d in range(32):
            if d:
                q = rcopy(send.at[d], recv.at[d], xss.at[d], xrs.at[d], (s + d) % 32, z)
                q.wait()
                v = recv[d].astype(F32)
            else:
                v = send[0].astype(F32)
            second_part = v * v[:, KV : KV + 1]
            b = b + second_part
            a = a + (v - second_part)
        part[0, 0] = a + rz[0, 0].astype(F32)
        part[0, 1] = b + rz[1, 0].astype(F32)
        for d in (1, 2, 3):
            rcopy(part.at[0], part.at[d], fss.at[d - 1], frs.at[d - 1], s, (z + d) % 4).start()

    def finish():
        for d in (1, 2, 3):
            rcopy(part.at[0], part.at[d], fss.at[d - 1], frs.at[d - 1], s, (z + d) % 4).wait()
        q = 2 * (z % 2)
        gc[0:16] = part[(z - q + 4) % 4, z // 2][:, :KV]
        gc[16:32] = part[(z - q + 3) % 4, z // 2][:, :KV]

    return head_send, head_relay, head_sum, spread, collect, finish


CACHE_SCRATCH = [
    pltpu.VMEM((4, 2, 4, 16, KP), BF),
    pltpu.VMEM((4, 2, 8, 16, KP), BF),
    pltpu.VMEM((2, 17, 16, KP), BF),
    pltpu.VMEM((32, 16, KP), BF),
    pltpu.VMEM((32, 16, KP), BF),
    pltpu.VMEM((4, 2, 16, KP), F32),
    pltpu.SemaphoreType.DMA((4, 2, 2)),
    pltpu.SemaphoreType.DMA((4, 2, 2)),
    pltpu.SemaphoreType.DMA((32,)),
    pltpu.SemaphoreType.DMA((32,)),
    pltpu.SemaphoreType.DMA((3,)),
    pltpu.SemaphoreType.DMA((3,)),
]

PHASES = [("fwd", 8, 4.0), ("ds0", 8, 0.6), ("kv0", 4, 1.6), ("ds1", 8, 0.6), ("kv1", 4, 1.6), ("dq", 8, 1.0)]
UV_GAP = 3.2
HEAD_GAP = 5.0


def plan():
    ends, now = [], 0.0
    for name, n, us in PHASES:
        for i in range(n):
            now += us
            ends.append((now, name, i))
    when = {(name, i): t for t, name, i in ends}
    todo = []
    for k in range(NCH):
        ready = when["fwd", 8 // NCH * (k + 1) - 1]
        for st in range(11):
            todo.append((ready + st * UV_GAP, "uv", (k, st)))
    for u in range(4):
        ready = when["kv%d" % (u // 2), 1 + 2 * (u % 2)]
        todo.append((ready, "head_send", (u,)))
        todo.append((ready + HEAD_GAP, "head_relay", (u,)))
        todo.append((ready + 2 * HEAD_GAP, "head_sum", (u,)))
    todo.sort(key=lambda e: e[0])
    at, late = {}, []
    for t, op, arg in todo:
        for end, name, i in ends:
            if end >= t - 1e-6:
                at.setdefault((name, i), []).append((op, arg))
                break
        else:
            late.append((op, arg))
    return at, late


def fused_body(lists, inv, flag, cache, qt, w_hbm, gout_hbm, ho_hbm, dq_hbm, uv_hbm, gc, *scr):
    qg, k, kt, mask, pt, do, cen, ot, gk, u, w, gout, hb, qb, lsem, hsem, qsem, osem = scr[:18]
    scr = scr[18:]
    gat = Gather(cache, *scr[: len(GATHER_SCRATCH)])
    full = gat.full
    scr = scr[len(GATHER_SCRATCH) :]
    stage = uv_stages(u, u, *scr[: len(UV_SCRATCH)])
    cs = cache_stages(inv, flag, gk, gc, *scr[len(UV_SCRATCH) :])
    head_send, head_relay, head_sum, spread, collect, finish = cs
    s, z, c, x, y = place()

    loads = [pltpu.make_async_copy(w_hbm, w, lsem.at[0]), pltpu.make_async_copy(gout_hbm, gout, lsem.at[1])]
    for q in loads:
        q.start()

    def q_load(i, slot):
        return pltpu.make_async_copy(qt.at[pl.ds(4 * i, 4)], qb.at[slot], qsem.at[slot])

    q_load(0, 0).start()
    q_load(1, 1).start()
    greet(range(1, 32), (1, 2, 3))
    gat.step0()
    make_mask(mask)
    row = lax.broadcasted_iota(jnp.int32, (64, ROWS), 0)
    one = jnp.where(row == 0, 1.0, 0.0).astype(BF)
    qg[0, KV:, :] = one
    qg[1, KV:, :] = one
    gat.step1()

    def prep_q(lo, hi):
        def body(i, _):
            q_load(i, i % 2).wait()
            for p in range(2):
                a, b = halves(qb[i % 2, 2 * p], qb[i % 2, 2 * p + 1])
                col = pl.ds(pl.multiple_of(i * TILE + p * 128, 128), 128)
                qg[0, :KV, col] = a
                qg[1, :KV, col] = b

            @pl.when(i + 2 < NT)
            def _():
                q_load(i + 2, i % 2).start()

            return 0

        lax.fori_loop(lo, hi, body, 0)

    def prep_do(lo, hi):
        def body(i, _):
            d0 = lax.dot_general(w[2 * i], gout[2 * i], NTD, preferred_element_type=F32).astype(BF)
            d1 = lax.dot_general(w[2 * i + 1], gout[2 * i + 1], NTD, preferred_element_type=F32).astype(BF)
            a, b = halves(d0, d1)
            col = pl.ds(pl.multiple_of(i * 128, 128), 128)
            do[0, :, col] = a
            do[1, :, col] = b
            return 0

        lax.fori_loop(lo, hi, body, 0)

    prep_q(0, 4)
    gat.step2()
    prep_q(4, 8)
    gat.step3()
    for q in loads:
        q.wait()
    prep_do(0, 8)
    gat.step4()
    prep_do(8, 16)
    gat.step5()
    gat.step6()
    gat.step7()

    colid = lax.broadcasted_iota(jnp.int32, (BLK, KP - DL), 1)
    for g in range(2):
        for j in range(SLOTS):
            if j == 0:
                blk = full[2 * s + g]
                bias = jnp.float32(0.0)
            else:
                e = lists[g, j - 1]
                blk = full[jnp.maximum(e, 0)]
                bias = jnp.where(e >= 0, 0.0, NEG).astype(F32)
            k[g, j * BLK : (j + 1) * BLK, :DL] = blk[:, :DL]
            rot = jnp.concatenate([blk[:, DL:].astype(F32), jnp.zeros((BLK, 64), F32)], 1)
            k[g, j * BLK : (j + 1) * BLK, DL:] = jnp.where(colid == 64, bias, rot).astype(BF)
        for b in range(8):
            kt[g, :, b * 128 : (b + 1) * 128] = jnp.swapaxes(k[g, b * 128 : (b + 1) * 128, :], 0, 1)

    uv_out = [pltpu.make_async_copy(u.at[q], uv_hbm.at[q], osem.at[q]) for q in range(NCH)]

    def run(op, arg):
        if op == "uv":
            stage(*arg)
            if arg[1] == 10:
                uv_out[arg[0]].start()
        else:
            {"head_send": head_send, "head_relay": head_relay, "head_sum": head_sum}[op](*arg)

    at, late = plan()

    def loop(name, body):
        n = {p[0]: p[1] for p in PHASES}[name]

        def step(i, _):
            body(i)
            for j in range(n):
                if (name, j) in at:

                    @pl.when(i == j)
                    def _():
                        for op, arg in at[name, j]:
                            run(op, arg)

            return 0

        lax.fori_loop(0, n, step, 0)

    def cols(i):
        return pl.ds(pl.multiple_of(i * TILE, TILE), TILE)

    def ho_store(i, slot):
        return pltpu.make_async_copy(hb.at[slot], ho_hbm.at[pl.ds(4 * i, 4)], hsem.at[slot])

    def fwd(i):
        col = cols(i)
        for g in range(2):
            sc = jnp.dot(k[g], qg[g, :, col], preferred_element_type=F32)
            sc = jnp.concatenate([sc[:BLK] + mask[...], sc[BLK:]], 0)
            m = jnp.max(sc, axis=0, keepdims=True)
            e = jnp.exp2((sc - m) * (SC * L2E))
            inv_l = 1.0 / jnp.sum(e, axis=0, keepdims=True)
            pb = e.astype(BF)
            pt[g, :, col] = pb
            o = jnp.dot(kt[g, :DL, :], pb, preferred_element_type=F32) * inv_l
            ot[g] = o.astype(BF)
            dn = (do[g, :, col].astype(F32) * inv_l).astype(BF)
            do[g, :, col] = dn
            centre = jnp.sum(o * dn.astype(F32), axis=0, keepdims=True)
            cen[g, :, col] = jnp.broadcast_to(centre, (8, TILE))

        @pl.when(i >= 2)
        def _():
            ho_store(i - 2, i % 2).wait()

        for p in range(2):
            hh = halves(ot[0, :, p * 128 : (p + 1) * 128], ot[1, :, p * 128 : (p + 1) * 128])
            for q in range(2):
                h = i * 4 + 2 * p + q
                part = jnp.dot(hh[q], gout[h], preferred_element_type=F32).astype(BF)
                per = CROWS // DL
                u[h // per, pl.ds(pl.multiple_of(h % per * DL, DL), DL)] = part
                hb[i % 2, 2 * p + q] = lax.dot_general(hh[q], w[h], TND, preferred_element_type=F32).astype(BF)
        ho_store(i, i % 2).start()

    loop("fwd", fwd)
    ho_store(6, 0).wait()
    ho_store(7, 1).wait()

    def back_ds(g, to):
        def body(i):
            col = cols(i)
            dp = jnp.dot(k[g, :, :DL], do[g, :, col], preferred_element_type=F32)
            t = pt[g, :, col].astype(F32) * (dp - cen[g, 0:1, col])
            pt[to, :, col] = t.astype(BF)

        return body

    def back_kv(g, d):
        def body(i):
            rows = cols(i)
            a = lax.dot_general(qg[g, :KV, :], pt[d, rows, :], NTD, preferred_element_type=F32) * SC
            b = lax.dot_general(do[g], pt[g, rows, :], NTD, preferred_element_type=F32)
            t = jnp.concatenate([a[:DL] + b, a[DL:], jnp.zeros((KP - KV, TILE), F32)], 0)
            t = jnp.swapaxes(t, 0, 1).astype(BF)
            gk[g, pl.ds(4 * i, 4)] = t.reshape(4, 4, 16, KP)

        return body

    loop("ds0", back_ds(0, 2))
    loop("kv0", back_kv(0, 2))
    loop("ds1", back_ds(1, 0))
    loop("kv1", back_kv(1, 0))

    def dq_store(i, slot):
        return pltpu.make_async_copy(qb.at[slot], dq_hbm.at[pl.ds(4 * i, 4)], qsem.at[slot])

    def back_q(i):
        col = cols(i)

        @pl.when(i >= 2)
        def _():
            dq_store(i - 2, i % 2).wait()

        r = []
        for g, d in ((0, 2), (1, 0)):
            r.append((jnp.dot(kt[g, :KV, :], pt[d, :, col], preferred_element_type=F32) * SC).astype(BF))
        for p in range(2):
            a, b = halves(r[0][:, p * 128 : (p + 1) * 128], r[1][:, p * 128 : (p + 1) * 128])
            qb[i % 2, 2 * p] = a
            qb[i % 2, 2 * p + 1] = b
        dq_store(i, i % 2).start()

    loop("dq", back_q)
    for op, arg in late:
        run(op, arg)
    spread()
    collect()
    finish()
    dq_store(6, 0).wait()
    dq_store(7, 1).wait()
    for q in uv_out:
        q.wait()


def attention(lists, inv, flag, cache, qt, w, gout):
    v = pl.BlockSpec(memory_space=pltpu.VMEM)
    m = pl.BlockSpec(memory_space=pltpu.SMEM)
    a = pl.BlockSpec(memory_space=pl.ANY)
    scratch = [
        pltpu.VMEM((2, KP, ROWS), BF),
        pltpu.VMEM((2, KEYS, KP), BF),
        pltpu.VMEM((2, KP, KEYS), BF),
        pltpu.VMEM((BLK, TILE), F32),
        pltpu.VMEM((3, KEYS, ROWS), BF),
        pltpu.VMEM((2, DL, ROWS), BF),
        pltpu.VMEM((2, 8, ROWS), F32),
        pltpu.VMEM((2, DL, TILE), BF),
        pltpu.VMEM((2, 16, 4, 16, KP), BF),
        pltpu.VMEM((NCH, CROWS, 128), BF),
        pltpu.VMEM((NH, DL, VH), BF),
        pltpu.VMEM((NH, TD, VH), BF),
        pltpu.VMEM((2, 4, TD, VH), BF),
        pltpu.VMEM((2, 4, KV, TD), BF),
        pltpu.SemaphoreType.DMA((2,)),
        pltpu.SemaphoreType.DMA((2,)),
        pltpu.SemaphoreType.DMA((2,)),
        pltpu.SemaphoreType.DMA((NCH,)),
    ]
    return pl.pallas_call(
        fused_body,
        out_shape=(
            jax.ShapeDtypeStruct((NH, TD, VH), BF),
            jax.ShapeDtypeStruct((NH, KV, TD), BF),
            jax.ShapeDtypeStruct((NCH, CROWS, 128), BF),
            jax.ShapeDtypeStruct((32, KV), F32),
        ),
        in_specs=[m, m, m, v, a, a, a],
        out_specs=(a, a, a, v),
        scratch_shapes=scratch + GATHER_SCRATCH + UV_SCRATCH + CACHE_SCRATCH,
        compiler_params=pltpu.CompilerParams(
            collective_id=0, has_side_effects=True, vmem_limit_bytes=63 * 2**20
        ),
        name="latent_attention",
    )(lists, inv, flag, cache, qt, w, gout)


def on_device(queries, cache, lists, w_uv, grad_out):
    shard = jnp.where(lists >= 0, lists // 2, -1)
    hit = shard[:, None, :] == jnp.arange(32)[None, :, None]
    inv = jnp.min(jnp.where(hit, jnp.arange(1, 16), 16), axis=-1).astype(jnp.int32)
    flag = jnp.max(jnp.where(hit, (lists % 2)[:, None, :], 0), axis=(0, 2)).astype(F32)
    ho, dq, uv, gc = attention(
        lists, inv, flag, cache, queries.transpose(1, 2, 0), w_uv, grad_out.transpose(1, 0, 2)
    )
    return ho.transpose(1, 0, 2), dq.transpose(2, 0, 1), gc, uv.reshape(NH, DL, VH)


def solution(mesh):
    return jax.shard_map(
        on_device,
        mesh=mesh,
        in_specs=(
            P("seq", "head", None),
            P(("seq", "head"), None),
            P("seq", None),
            P("head", None, None),
            P("seq", "head", None),
        ),
        out_specs=(
            P("seq", "head", None),
            P("seq", "head", None),
            P(("seq", "head"), None),
            P("head", None, None),
        ),
        check_vma=False,
    )
```

time: 184 us -> 153 us (0.83)
  Pallas kernels: 173 us -> 137 us
  local copies, waits for them, and re-layouts: 9.41 us -> 13.3 us
    pallas_call x3 -> x1, Pallas kernels: 173 us -> 137 us  [attention(): pl.pallas_call(fused_body, out_shape=(jax.ShapeDtypeStruct((NH, TD, VH),...]
    unnamed x10 -> x9, local copies, waits for them, and re-layouts: 9.22 us -> 13.1 us
where the time goes in v2:
time: 153 us
  Pallas kernels  137 us (90%)
  local copies, waits for them, and re-layouts  13.3 us (9%)
  other arithmetic  1.89 us (1%)
    pallas_call x1, Pallas kernels, attention(): pl.pallas_call(fused_body, out_shape=(jax.ShapeDtypeStruct((NH, TD, VH),...  137 us
    unnamed x9, local copies, waits for them, and re-layouts  13.1 us

profile of v2, /device:TPU:1, one launch (start us, length us, event | category | flops | bytes accessed | tf_op | source)
XLA Modules:
  0.0 153.1 jit_solution(14086095578454610928)
XLA Ops:
  0.6 0.7 compare_select_fusion
  1.3 0.1 copy.11
  1.4 0.1 copy.12
  1.5 0.7 select_reduce_fusion
  2.2 0.5 convert_element_type.3.flag
  2.7 2.6 %copy.16 = bf16[128,32,128]{2,0,1:T(8,128)(2,1)} copy(bf16[128,32,128]{2,1,0:T(8,128)(2,1)} %param.9) | data formatting | bytes 2097152 | tf_op args[4]
  5.3 137.3 %latent_attention.1 = (bf16[32,128,128]{2,1,0:T(8,128)(2,1)}, bf16[32,576,128]{2,1,0:T(8,128)(2,1)}, bf16[4,4096,128]{2,1,0:T(8,128)(2,1)}, f32[32,576]{1,0:T(8,128)}) custom-call(s32[2,15]{1,0:T(2,128)} %lists.1, s32[2,32]{1,0:T(2,128)} %get-tuple-element.21.inv, f32[32]{0:T(128)} %convert_element_type.3.flag, bf16[32,576]{1,0:T(8,128)(2,1)} %cache.1, ...), custom_call_target="tpu_custom_call" | custom-call | tf_op jit(solution)/shard_map/latent_attention/pallas_call | solution.py:685
  142.6 2.9 %copy.14 = bf16[128,32,128]{2,1,0:T(8,128)(2,1)} copy(bf16[128,32,128]{2,0,1:T(8,128)(2,1)} %bitcast.11) | data formatting | bytes 2097152
  145.5 0.0 copy-start.1
  145.5 0.0 copy-start
  145.5 5.0 %copy.20 = bf16[128,32,576]{0,2,1:T(8,128)(2,1)} copy(bf16[128,32,576]{0,2,1:T(8,128)(2,1)} %bitcast.8) | data formatting | bytes 9437184
  150.5 0.0 copy-done.1
  150.5 0.6 copy.21
  151.1 0.0 copy-done
  151.1 2.0 %copy.22 = bf16[32,512,128]{2,1,0:T(8,128)(2,1)} copy(bf16[32,512,128]{2,1,0:T(8,128)(2,1)S(1)} %bitcast.10) | data formatting | bytes 8388608
  (1 shorter events, 0.0 us)
Async XLA Ops:
  145.5 5.0 %copy-start.1 = (f32[32,576]{1,0:T(8,128)S(1)}, f32[32,576]{1,0:T(8,128)}, u32[]{:S(2)}) copy-start(f32[32,576]{1,0:T(8,128)} %get-tuple-element.30) | copy-start | bytes 221188
  145.5 5.6 %copy-start = (bf16[4,4096,128]{2,1,0:T(8,128)(2,1)S(1)}, bf16[4,4096,128]{2,1,0:T(8,128)(2,1)}, u32[]{:S(2)}) copy-start(bf16[4,4096,128]{2,1,0:T(8,128)(2,1)} %get-tuple-element.11) | copy-start | bytes 12582916

commit v3 on v2

--- a/solution.py
+++ b/solution.py
@@ -198,6 +198,10 @@
 ]
 
 
+VMEM_LIMIT = 63 * 2**20
+WIDE = 512
+
+
 class Gather:
     def __init__(self, cache_ref, full, lsem, zs, zr, s1, r1, s2, r2, s3, r3, s4, r4, s5, r5):
         self.__dict__.update(locals())
@@ -235,18 +239,32 @@
         k = (a % 4) * 4 + b % 4
         self.start(self.at(a, b), self.s5.at[k], self.r5.at[k], seq_at(y, x, 1 - c))
 
+    def send_part(self, a, b, part, side, sems, nbr):
+        ssem, rsem = sems
+        self.start(self.at(a, b, part), ssem.at[side, part], rsem.at[side, part], nbr(1 - 2 * side))
+
+    def first_sends(self, a, b, sems, nbr):
+        self.send_part(a, b, 0, 0, sems, nbr)
+        self.send_part(a, b, 1, 1, sems, nbr)
+        self.send_part(a, b, 1, 0, sems, nbr)
+        self.send_part(a, b, 0, 1, sems, nbr)
+
     def b_sends(self, a):
         k = a % 4
-        self.start(self.at(a, 0), self.s3.at[k, 0], self.r3.at[k, 0], self.nbr_b(1))
-        self.start(self.at(a, 0), self.s3.at[k, 1], self.r3.at[k, 1], self.nbr_b(-1))
+        self.first_sends(a, 0, (self.s3.at[k], self.r3.at[k]), self.nbr_b)
 
     def b_relay(self, a):
         k = a % 4
-        self.got(self.at(a, -1), self.r3.at[k, 0])
+        self.got(self.at(a, -1, 0), self.r3.at[k, 0, 0])
         self.start(self.at(a, -1, 0), self.s4.at[k, 0], self.r4.at[k, 0], self.nbr_b(1))
-        self.got(self.at(a, 1), self.r3.at[k, 1])
+        self.got(self.at(a, 1, 1), self.r3.at[k, 1, 1])
         self.start(self.at(a, 1, 1), self.s4.at[k, 1], self.r4.at[k, 1], self.nbr_b(-1))
+
+    def b_rest(self, a):
+        k = a % 4
+        self.got(self.at(a, -1, 1), self.r3.at[k, 0, 1])
         self.to_twin(a, -1)
+        self.got(self.at(a, 1, 0), self.r3.at[k, 1, 0])
         self.to_twin(a, 1)
 
     def step0(self):
@@ -265,16 +283,17 @@
         self.local.wait()
         for q in self.zc:
             q.wait_recv()
-        self.start(self.at(0, 0), self.s1.at[0], self.r1.at[0], self.nbr_a(1))
-        self.start(self.at(0, 0), self.s1.at[1], self.r1.at[1], self.nbr_a(-1))
+        self.first_sends(0, 0, (self.s1, self.r1), self.nbr_a)
         self.b_sends(0)
         self.to_twin(0, 0)
 
     def step2(self):
-        self.got(self.at(-1, 0), self.r1.at[0])
+        self.got(self.at(-1, 0, 0), self.r1.at[0, 0])
         self.start(self.at(-1, 0, 0), self.s2.at[0], self.r2.at[0], self.nbr_a(1))
-        self.got(self.at(1, 0), self.r1.at[1])
+        self.got(self.at(1, 0, 1), self.r1.at[1, 1])
         self.start(self.at(1, 0, 1), self.s2.at[1], self.r2.at[1], self.nbr_a(-1))
+        self.got(self.at(-1, 0, 1), self.r1.at[0, 1])
+        self.got(self.at(1, 0, 0), self.r1.at[1, 0])
         self.b_sends(-1)
         self.b_sends(1)
         self.to_twin(-1, 0)
@@ -285,14 +304,18 @@
         self.got(self.at(2, 0, 0), self.r2.at[0])
         self.got(self.at(2, 0, 1), self.r2.at[1])
         self.b_sends(2)
+        self.b_rest(0)
         self.to_twin(2, 0)
 
     def step4(self):
         for a in (-1, 1):
             self.b_relay(a)
+        for a in (-1, 1):
+            self.b_rest(a)
 
     def step5(self):
         self.b_relay(2)
+        self.b_rest(2)
 
     def step6(self):
         for a in (0, -1, 1, 2):
@@ -313,7 +336,7 @@
 
 GATHER_SCRATCH = [pltpu.VMEM((64, BLK, KV), BF), pltpu.SemaphoreType.DMA] + [
     pltpu.SemaphoreType.DMA(shape)
-    for shape in ((3,), (3,), (2,), (2,), (2,), (2,), (4, 2), (4, 2), (4, 2), (4, 2), (16,), (16,))
+    for shape in ((3,), (3,), (2, 2), (2, 2), (2,), (2,), (4, 2, 2), (4, 2, 2), (4, 2), (4, 2), (16,), (16,))
 ]
 
 
@@ -321,18 +344,21 @@
     s, z, c, x, y = place()
     z1, z2, z3 = (z + 1) % 4, (z + 2) % 4, (z + 3) % 4
 
+    def quarter(b, n, q):
+        return gk.at[pl.ds(b, n), pl.ds(pl.multiple_of(q * 16, 16), 16)]
+
     def first(u):
-        g, b = u // 2, u % 2 * 8
+        b = 8 * u
         return [
-            rcopy(gk.at[g, b : b + 4, z2], zr1.at[u, 0], zss.at[u, 0, 0], zrs.at[u, 0, 0], s, z1),
-            rcopy(gk.at[g, b + 4 : b + 8, z2], zr1.at[u, 1], zss.at[u, 0, 1], zrs.at[u, 0, 1], s, z3),
+            rcopy(quarter(b, 4, z2), zr1.at[u, 0], zss.at[u, 0, 0], zrs.at[u, 0, 0], s, z1),
+            rcopy(quarter(b + 4, 4, z2), zr1.at[u, 1], zss.at[u, 0, 1], zrs.at[u, 0, 1], s, z3),
         ]
 
     def second(u):
-        g, b = u // 2, u % 2 * 8
+        b = 8 * u
         return [
-            rcopy(gk.at[g, b : b + 8, z1], zr2.at[u, 0], zss.at[u, 1, 0], zrs.at[u, 1, 0], s, z1),
-            rcopy(gk.at[g, b : b + 8, z3], zr2.at[u, 1], zss.at[u, 1, 1], zrs.at[u, 1, 1], s, z3),
+            rcopy(quarter(b, 8, z1), zr2.at[u, 0], zss.at[u, 1, 0], zrs.at[u, 1, 0], s, z1),
+            rcopy(quarter(b, 8, z3), zr2.at[u, 1], zss.at[u, 1, 1], zrs.at[u, 1, 1], s, z3),
         ]
 
     def head_send(u):
@@ -340,45 +366,43 @@
             q.start()
 
     def head_relay(u):
-        g, b = u // 2, u % 2 * 8
+        b = 8 * u
         for q in first(u):
             q.wait()
-        gk[g, b : b + 4, z1] = (gk[g, b : b + 4, z1].astype(F32) + zr1[u, 0].astype(F32)).astype(BF)
-        gk[g, b + 4 : b + 8, z3] = (gk[g, b + 4 : b + 8, z3].astype(F32) + zr1[u, 1].astype(F32)).astype(BF)
+        for r, b0, q in ((zr1.at[u, 0], b, z1), (zr1.at[u, 1], b + 4, z3)):
+            t = quarter(b0, 4, q)
+            t[...] = (t[...].astype(F32) + r[...].astype(F32)).astype(BF)
         for q in second(u):
             q.start()
 
     def head_sum(u):
-        g, b = u // 2, u % 2 * 8
         for q in second(u):
             q.wait()
-        t = gk[g, b : b + 8, z].astype(F32) + zr2[u, 0].astype(F32) + zr2[u, 1].astype(F32)
-        rz[g, b : b + 8] = t.astype(BF)
-        if b:
-            rz[g, 16] = jnp.zeros((16, KP), BF)
-
-    col = lax.broadcasted_iota(jnp.int32, (16, KP), 1)
+        t = quarter(8 * u, 8, z)[...].astype(F32) + zr2[u, 0].astype(F32) + zr2[u, 1].astype(F32)
+        rz[u // 2, 8 * (u % 2) : 8 * (u % 2) + 8] = t.astype(BF)
+        if u % 2:
+            rz[u // 2, 16] = jnp.zeros((16, KV), BF)
 
     def spread():
         for d in range(32):
             t = (s + d) % 32
             v = rz[0, inv[0, t]].astype(F32) + rz[1, inv[1, t]].astype(F32)
-            v = jnp.where(col == KV, flag[t], v)
-            send[d] = v.astype(BF)
+            mark = jnp.zeros((16, KP - KV), F32) + flag[t].astype(F32)
+            send[d] = jnp.concatenate([v, mark], 1).astype(BF)
             if d:
                 rcopy(send.at[d], recv.at[d], xss.at[d], xrs.at[d], t, z).start()
 
     def collect():
-        a = jnp.zeros((16, KP), F32)
-        b = jnp.zeros((16, KP), F32)
+        a = jnp.zeros((16, KV), F32)
+        b = jnp.zeros((16, KV), F32)
         for d in range(32):
             if d:
-                q = rcopy(send.at[d], recv.at[d], xss.at[d], xrs.at[d], (s + d) % 32, z)
-                q.wait()
+                rcopy(send.at[d], recv.at[d], xss.at[d], xrs.at[d], (s + d) % 32, z).wait()
                 v = recv[d].astype(F32)
             else:
                 v = send[0].astype(F32)
-            second_part = v * v[:, KV : KV + 1]
+            v, mark = v[:, :KV], v[:, KV : KV + 1]
+            second_part = v * mark
             b = b + second_part
             a = a + (v - second_part)
         part[0, 0] = a + rz[0, 0].astype(F32)
@@ -390,19 +414,19 @@
         for d in (1, 2, 3):
             rcopy(part.at[0], part.at[d], fss.at[d - 1], frs.at[d - 1], s, (z + d) % 4).wait()
         q = 2 * (z % 2)
-        gc[0:16] = part[(z - q + 4) % 4, z // 2][:, :KV]
-        gc[16:32] = part[(z - q + 3) % 4, z // 2][:, :KV]
+        gc[0:16] = part[(z - q + 4) % 4, z // 2]
+        gc[16:32] = part[(z - q + 3) % 4, z // 2]
 
     return head_send, head_relay, head_sum, spread, collect, finish
 
 
 CACHE_SCRATCH = [
-    pltpu.VMEM((4, 2, 4, 16, KP), BF),
-    pltpu.VMEM((4, 2, 8, 16, KP), BF),
-    pltpu.VMEM((2, 17, 16, KP), BF),
+    pltpu.VMEM((4, 2, 4, 16, KV), BF),
+    pltpu.VMEM((4, 2, 8, 16, KV), BF),
+    pltpu.VMEM((2, 17, 16, KV), BF),
     pltpu.VMEM((32, 16, KP), BF),
     pltpu.VMEM((32, 16, KP), BF),
-    pltpu.VMEM((4, 2, 16, KP), F32),
+    pltpu.VMEM((4, 2, 16, KV), F32),
     pltpu.SemaphoreType.DMA((4, 2, 2)),
     pltpu.SemaphoreType.DMA((4, 2, 2)),
     pltpu.SemaphoreType.DMA((32,)),
@@ -411,9 +435,9 @@
     pltpu.SemaphoreType.DMA((3,)),
 ]
 
-PHASES = [("fwd", 8, 4.0), ("ds0", 8, 0.6), ("kv0", 4, 1.6), ("ds1", 8, 0.6), ("kv1", 4, 1.6), ("dq", 8, 1.0)]
+PHASES = [("fwd", 8, 2.3), ("ds0", 2, 1.3), ("kv0", 2, 2.6), ("ds1", 2, 1.3), ("kv1", 2, 2.6), ("dq", 4, 1.5)]
 UV_GAP = 3.2
-HEAD_GAP = 5.0
+HEAD_GAP = 4.0
 
 
 def plan():
@@ -429,7 +453,7 @@
         for st in range(11):
             todo.append((ready + st * UV_GAP, "uv", (k, st)))
     for u in range(4):
-        ready = when["kv%d" % (u // 2), 1 + 2 * (u % 2)]
+        ready = when["kv%d" % (u // 2), u % 2]
         todo.append((ready, "head_send", (u,)))
         todo.append((ready + HEAD_GAP, "head_relay", (u,)))
         todo.append((ready + 2 * HEAD_GAP, "head_sum", (u,)))
@@ -445,45 +469,79 @@
     return at, late
 
 
-def fused_body(lists, inv, flag, cache, qt, w_hbm, gout_hbm, ho_hbm, dq_hbm, uv_hbm, gc, *scr):
-    qg, k, kt, mask, pt, do, cen, ot, gk, u, w, gout, hb, qb, lsem, hsem, qsem, osem = scr[:18]
-    scr = scr[18:]
+def fused_body(lists, cache, qt, w_hbm, gout_hbm, ho_hbm, dq_hbm, uv_hbm, gc, *scr):
+    (qg, k, kt, mask, pt, do, cen, ot, sa, sb, u, w, gout, hb, qb, inv, flag,
+     lsem, hsem, qsem, osem) = scr[:21]
+    scr = scr[21:]
     gat = Gather(cache, *scr[: len(GATHER_SCRATCH)])
     full = gat.full
     scr = scr[len(GATHER_SCRATCH) :]
     stage = uv_stages(u, u, *scr[: len(UV_SCRATCH)])
+    gk = full
     cs = cache_stages(inv, flag, gk, gc, *scr[len(UV_SCRATCH) :])
     head_send, head_relay, head_sum, spread, collect, finish = cs
     s, z, c, x, y = place()
 
-    loads = [pltpu.make_async_copy(w_hbm, w, lsem.at[0]), pltpu.make_async_copy(gout_hbm, gout, lsem.at[1])]
-    for q in loads:
-        q.start()
+    barrier = pltpu.get_barrier_semaphore()
+    for d in range(1, 32):
+        pl.semaphore_signal(barrier, inc=1, device_id=((s + d) % 32, z), device_id_type=MESH)
+    for d in range(1, 4):
+        pl.semaphore_signal(barrier, inc=1, device_id=(s, (z + d) % 4), device_id_type=MESH)
 
     def q_load(i, slot):
-        return pltpu.make_async_copy(qt.at[pl.ds(4 * i, 4)], qb.at[slot], qsem.at[slot])
-
+        return pltpu.make_async_copy(qt.at[pl.ds(8 * i, 8)], qb.at[slot], qsem.at[slot])
+
+    g_load = pltpu.make_async_copy(gout_hbm, u.at[0], lsem.at[1])
+    w_load = pltpu.make_async_copy(w_hbm, w, lsem.at[0])
+    g_load.start()
     q_load(0, 0).start()
     q_load(1, 1).start()
-    greet(range(1, 32), (1, 2, 3))
-    gat.step0()
-    make_mask(mask)
+    w_load.start()
+
+    r = lax.broadcasted_iota(jnp.int32, (BLK, WIDE), 0)
+    cc = lax.broadcasted_iota(jnp.int32, (BLK, WIDE), 1)
+    mask[...] = jnp.where(r <= (cc % BLK), 0.0, NEG).astype(F32)
     row = lax.broadcasted_iota(jnp.int32, (64, ROWS), 0)
     one = jnp.where(row == 0, 1.0, 0.0).astype(BF)
     qg[0, KV:, :] = one
     qg[1, KV:, :] = one
+    pl.semaphore_wait(barrier, 34)
+    gat.step0()
+
+    def find(t, _):
+        which = jnp.int32(0)
+        for g in range(2):
+            slot = jnp.int32(16)
+            for j in range(KEEP):
+                d = lists[g, j] - 2 * t
+                hit = (d >= 0) & (d < 2)
+                slot = jnp.where(hit, j + 1, slot)
+                which = jnp.where(hit, d, which)
+            inv[g, t] = slot
+        flag[t] = which
+        return 0
+
+    g_load.wait()
+
+    def turn(i, _):
+        t = pl.ds(pl.multiple_of(i * 16, 16), 16)
+        x = u[0, pl.ds(pl.multiple_of(i * 512, 512), 512)].reshape(16, NH, VH)
+        gout[:, t, :] = jnp.swapaxes(x, 0, 1)
+        return 0
+
+    lax.fori_loop(0, TD // 16, turn, 0)
     gat.step1()
 
     def prep_q(lo, hi):
         def body(i, _):
             q_load(i, i % 2).wait()
-            for p in range(2):
+            for p in range(4):
                 a, b = halves(qb[i % 2, 2 * p], qb[i % 2, 2 * p + 1])
-                col = pl.ds(pl.multiple_of(i * TILE + p * 128, 128), 128)
+                col = pl.ds(pl.multiple_of(i * WIDE + p * 128, 128), 128)
                 qg[0, :KV, col] = a
                 qg[1, :KV, col] = b
 
-            @pl.when(i + 2 < NT)
+            @pl.when(i + 2 < 4)
             def _():
                 q_load(i + 2, i % 2).start()
 
@@ -493,26 +551,28 @@
 
     def prep_do(lo, hi):
         def body(i, _):
-            d0 = lax.dot_general(w[2 * i], gout[2 * i], NTD, preferred_element_type=F32).astype(BF)
-            d1 = lax.dot_general(w[2 * i + 1], gout[2 * i + 1], NTD, preferred_element_type=F32).astype(BF)
-            a, b = halves(d0, d1)
-            col = pl.ds(pl.multiple_of(i * 128, 128), 128)
-            do[0, :, col] = a
-            do[1, :, col] = b
+            for p in range(4):
+                h = 8 * i + 2 * p
+                d0 = lax.dot_general(w[h], gout[h], NTD, preferred_element_type=F32).astype(BF)
+                d1 = lax.dot_general(w[h + 1], gout[h + 1], NTD, preferred_element_type=F32).astype(BF)
+                a, b = halves(d0, d1)
+                col = pl.ds(pl.multiple_of(i * WIDE + p * 128, 128), 128)
+                do[0, :, col] = a
+                do[1, :, col] = b
             return 0
 
         lax.fori_loop(lo, hi, body, 0)
 
-    prep_q(0, 4)
+    prep_q(0, 2)
     gat.step2()
-    prep_q(4, 8)
+    prep_q(2, 4)
     gat.step3()
-    for q in loads:
-        q.wait()
-    prep_do(0, 8)
+    w_load.wait()
+    prep_do(0, 2)
     gat.step4()
-    prep_do(8, 16)
+    prep_do(2, 4)
     gat.step5()
+    lax.fori_loop(0, 32, find, 0)
     gat.step6()
     gat.step7()
 
@@ -530,7 +590,8 @@
             rot = jnp.concatenate([blk[:, DL:].astype(F32), jnp.zeros((BLK, 64), F32)], 1)
             k[g, j * BLK : (j + 1) * BLK, DL:] = jnp.where(colid == 64, bias, rot).astype(BF)
         for b in range(8):
-            kt[g, :, b * 128 : (b + 1) * 128] = jnp.swapaxes(k[g, b * 128 : (b + 1) * 128, :], 0, 1)
+            t = jnp.swapaxes(k[g, b * 128 : (b + 1) * 128, :], 0, 1)
+            kt[g, :, b * 128 : (b + 1) * 128] = t[:KV]
 
     uv_out = [pltpu.make_async_copy(u.at[q], uv_hbm.at[q], osem.at[q]) for q in range(NCH)]
 
@@ -543,82 +604,102 @@
             {"head_send": head_send, "head_relay": head_relay, "head_sum": head_sum}[op](*arg)
 
     at, late = plan()
-
-    def loop(name, body):
-        n = {p[0]: p[1] for p in PHASES}[name]
-
+    steps = {p[0]: p[1] for p in PHASES}
+
+    def hook(name, i, part=0, parts=1):
+        for j in range(part, steps[name], parts):
+            if (name, j) in at:
+
+                @pl.when(i == j // parts)
+                def _():
+                    for op, arg in at[name, j]:
+                        run(op, arg)
+
+    def loop(name, body, parts=1):
         def step(i, _):
             body(i)
-            for j in range(n):
-                if (name, j) in at:
-
-                    @pl.when(i == j)
-                    def _():
-                        for op, arg in at[name, j]:
-                            run(op, arg)
-
+            hook(name, i, parts - 1, parts)
             return 0
 
-        lax.fori_loop(0, n, step, 0)
-
-    def cols(i):
-        return pl.ds(pl.multiple_of(i * TILE, TILE), TILE)
+        lax.fori_loop(0, steps[name] // parts, step, 0)
+
+    def cols(i, n=WIDE):
+        return pl.ds(pl.multiple_of(i * n, n), n)
 
     def ho_store(i, slot):
-        return pltpu.make_async_copy(hb.at[slot], ho_hbm.at[pl.ds(4 * i, 4)], hsem.at[slot])
+        return pltpu.make_async_copy(hb.at[slot], ho_hbm.at[pl.ds(8 * i, 8)], hsem.at[slot])
+
+    def scores(to, g, i):
+        to[...] = jnp.dot(k[g], qg[g, :, cols(i)], preferred_element_type=F32)
+
+    def softmax(sc, g, col):
+        sc[:BLK] = sc[:BLK] + mask[...]
+        m = jnp.max(sc[...], axis=0, keepdims=True)
+        total = jnp.zeros((8, WIDE), F32)
+        for b in range(16):
+            e = jnp.exp2((sc[b * 64 : (b + 1) * 64] - m) * (SC * L2E))
+            total = total + jnp.sum(e.reshape(8, 8, WIDE), axis=0)
+            pt[g, b * 64 : (b + 1) * 64, col] = e.astype(BF)
+        return 1.0 / jnp.sum(total, axis=0, keepdims=True)
+
+    def values(g, col, inv_l):
+        o = jnp.dot(kt[g, :DL, :], pt[g, :, col], preferred_element_type=F32) * inv_l
+        ot[g] = o.astype(BF)
+        dn = (do[g, :, col].astype(F32) * inv_l).astype(BF)
+        do[g, :, col] = dn
+        centre = jnp.sum(o * dn.astype(F32), axis=0, keepdims=True)
+        cen[g, :, col] = jnp.broadcast_to(centre, (8, WIDE))
+
+    scores(sa, 0, 0)
 
     def fwd(i):
         col = cols(i)
-        for g in range(2):
-            sc = jnp.dot(k[g], qg[g, :, col], preferred_element_type=F32)
-            sc = jnp.concatenate([sc[:BLK] + mask[...], sc[BLK:]], 0)
-            m = jnp.max(sc, axis=0, keepdims=True)
-            e = jnp.exp2((sc - m) * (SC * L2E))
-            inv_l = 1.0 / jnp.sum(e, axis=0, keepdims=True)
-            pb = e.astype(BF)
-            pt[g, :, col] = pb
-            o = jnp.dot(kt[g, :DL, :], pb, preferred_element_type=F32) * inv_l
-            ot[g] = o.astype(BF)
-            dn = (do[g, :, col].astype(F32) * inv_l).astype(BF)
-            do[g, :, col] = dn
-            centre = jnp.sum(o * dn.astype(F32), axis=0, keepdims=True)
-            cen[g, :, col] = jnp.broadcast_to(centre, (8, TILE))
+        scores(sb, 1, i)
+        values(0, col, softmax(sa, 0, col))
+        hook("fwd", i, 0, 2)
+        scores(sa, 0, jnp.minimum(i + 1, 3))
+        values(1, col, softmax(sb, 1, col))
 
         @pl.when(i >= 2)
         def _():
             ho_store(i - 2, i % 2).wait()
 
-        for p in range(2):
+        for p in range(4):
             hh = halves(ot[0, :, p * 128 : (p + 1) * 128], ot[1, :, p * 128 : (p + 1) * 128])
             for q in range(2):
-                h = i * 4 + 2 * p + q
-                part = jnp.dot(hh[q], gout[h], preferred_element_type=F32).astype(BF)
-                per = CROWS // DL
-                u[h // per, pl.ds(pl.multiple_of(h % per * DL, DL), DL)] = part
-                hb[i % 2, 2 * p + q] = lax.dot_general(hh[q], w[h], TND, preferred_element_type=F32).astype(BF)
+                h = 2 * p + q
+                part = jnp.dot(hh[q], gout[8 * i + h], preferred_element_type=F32).astype(BF)
+                u[i, h * DL : (h + 1) * DL] = part
+                hb[i % 2, h] = lax.dot_general(hh[q], w[8 * i + h], TND, preferred_element_type=F32).astype(BF)
         ho_store(i, i % 2).start()
 
-    loop("fwd", fwd)
-    ho_store(6, 0).wait()
-    ho_store(7, 1).wait()
+    loop("fwd", fwd, 2)
+    ho_store(2, 0).wait()
+    ho_store(3, 1).wait()
 
     def back_ds(g, to):
         def body(i):
-            col = cols(i)
-            dp = jnp.dot(k[g, :, :DL], do[g, :, col], preferred_element_type=F32)
-            t = pt[g, :, col].astype(F32) * (dp - cen[g, 0:1, col])
-            pt[to, :, col] = t.astype(BF)
+            for b, tmp in enumerate((sa, sb)):
+                col = cols(2 * i + b)
+                tmp[...] = jnp.dot(k[g, :, :DL], do[g, :, col], preferred_element_type=F32)
+            for b, tmp in enumerate((sa, sb)):
+                col = cols(2 * i + b)
+                for q in range(8):
+                    rows = slice(q * 128, (q + 1) * 128)
+                    t = pt[g, rows, col].astype(F32) * (tmp[rows] - cen[g, 0:1, col])
+                    pt[to, rows, col] = t.astype(BF)
 
         return body
 
     def back_kv(g, d):
         def body(i):
             rows = cols(i)
-            a = lax.dot_general(qg[g, :KV, :], pt[d, rows, :], NTD, preferred_element_type=F32) * SC
-            b = lax.dot_general(do[g], pt[g, rows, :], NTD, preferred_element_type=F32)
-            t = jnp.concatenate([a[:DL] + b, a[DL:], jnp.zeros((KP - KV, TILE), F32)], 0)
-            t = jnp.swapaxes(t, 0, 1).astype(BF)
-            gk[g, pl.ds(4 * i, 4)] = t.reshape(4, 4, 16, KP)
+            sa[:KV] = lax.dot_general(qg[g, :KV, :], pt[d, rows, :], NTD, preferred_element_type=F32)
+            sb[:DL] = lax.dot_general(do[g], pt[g, rows, :], NTD, preferred_element_type=F32)
+            zero = jnp.zeros((KP - KV, WIDE), F32)
+            t = jnp.concatenate([sa[:DL] * SC + sb[:DL], sa[DL:KV] * SC, zero], 0).astype(BF)
+            t = jnp.swapaxes(t, 0, 1)
+            gk[pl.ds(16 * g + 8 * i, 8)] = t[:, :KV].reshape(8, BLK, KV)
 
         return body
 
@@ -628,7 +709,7 @@
     loop("kv1", back_kv(1, 0))
 
     def dq_store(i, slot):
-        return pltpu.make_async_copy(qb.at[slot], dq_hbm.at[pl.ds(4 * i, 4)], qsem.at[slot])
+        return pltpu.make_async_copy(qb.at[slot], dq_hbm.at[pl.ds(8 * i, 8)], qsem.at[slot])
 
     def back_q(i):
         col = cols(i)
@@ -639,8 +720,8 @@
 
         r = []
         for g, d in ((0, 2), (1, 0)):
-            r.append((jnp.dot(kt[g, :KV, :], pt[d, :, col], preferred_element_type=F32) * SC).astype(BF))
-        for p in range(2):
+            r.append((jnp.dot(kt[g], pt[d, :, col], preferred_element_type=F32) * SC).astype(BF))
+        for p in range(4):
             a, b = halves(r[0][:, p * 128 : (p + 1) * 128], r[1][:, p * 128 : (p + 1) * 128])
             qb[i % 2, 2 * p] = a
             qb[i % 2, 2 * p + 1] = b
@@ -652,31 +733,34 @@
     spread()
     collect()
     finish()
-    dq_store(6, 0).wait()
-    dq_store(7, 1).wait()
+    dq_store(2, 0).wait()
+    dq_store(3, 1).wait()
     for q in uv_out:
         q.wait()
 
 
-def attention(lists, inv, flag, cache, qt, w, gout):
+def attention(lists, cache, qt, w, gout):
     v = pl.BlockSpec(memory_space=pltpu.VMEM)
     m = pl.BlockSpec(memory_space=pltpu.SMEM)
     a = pl.BlockSpec(memory_space=pl.ANY)
     scratch = [
         pltpu.VMEM((2, KP, ROWS), BF),
         pltpu.VMEM((2, KEYS, KP), BF),
-        pltpu.VMEM((2, KP, KEYS), BF),
-        pltpu.VMEM((BLK, TILE), F32),
+        pltpu.VMEM((2, KV, KEYS), BF),
+        pltpu.VMEM((BLK, WIDE), F32),
         pltpu.VMEM((3, KEYS, ROWS), BF),
         pltpu.VMEM((2, DL, ROWS), BF),
         pltpu.VMEM((2, 8, ROWS), F32),
-        pltpu.VMEM((2, DL, TILE), BF),
-        pltpu.VMEM((2, 16, 4, 16, KP), BF),
+        pltpu.VMEM((2, DL, WIDE), BF),
+        pltpu.VMEM((KEYS, WIDE), F32),
+        pltpu.VMEM((KEYS, WIDE), F32),
         pltpu.VMEM((NCH, CROWS, 128), BF),
         pltpu.VMEM((NH, DL, VH), BF),
         pltpu.VMEM((NH, TD, VH), BF),
-        pltpu.VMEM((2, 4, TD, VH), BF),
-        pltpu.VMEM((2, 4, KV, TD), BF),
+        pltpu.VMEM((2, 8, TD, VH), BF),
+        pltpu.VMEM((2, 8, KV, TD), BF),
+        pltpu.SMEM((2, 32), jnp.int32),
+        pltpu.SMEM((32,), jnp.int32),
         pltpu.SemaphoreType.DMA((2,)),
         pltpu.SemaphoreType.DMA((2,)),
         pltpu.SemaphoreType.DMA((2,)),
@@ -690,23 +774,19 @@
             jax.ShapeDtypeStruct((NCH, CROWS, 128), BF),
             jax.ShapeDtypeStruct((32, KV), F32),
         ),
-        in_specs=[m, m, m, v, a, a, a],
+        in_specs=[m, v, a, a, a],
         out_specs=(a, a, a, v),
         scratch_shapes=scratch + GATHER_SCRATCH + UV_SCRATCH + CACHE_SCRATCH,
         compiler_params=pltpu.CompilerParams(
-            collective_id=0, has_side_effects=True, vmem_limit_bytes=63 * 2**20
+            collective_id=0, has_side_effects=True, vmem_limit_bytes=VMEM_LIMIT
         ),
         name="latent_attention",
-    )(lists, inv, flag, cache, qt, w, gout)
+    )(lists, cache, qt, w, gout)
 
 
 def on_device(queries, cache, lists, w_uv, grad_out):
-    shard = jnp.where(lists >= 0, lists // 2, -1)
-    hit = shard[:, None, :] == jnp.arange(32)[None, :, None]
-    inv = jnp.min(jnp.where(hit, jnp.arange(1, 16), 16), axis=-1).astype(jnp.int32)
-    flag = jnp.max(jnp.where(hit, (lists % 2)[:, None, :], 0), axis=(0, 2)).astype(F32)
     ho, dq, uv, gc = attention(
-        lists, inv, flag, cache, queries.transpose(1, 2, 0), w_uv, grad_out.transpose(1, 0, 2)
+        lists, cache, queries.transpose(1, 2, 0), w_uv, grad_out.reshape(TD * NH, VH)
     )
     return ho.transpose(1, 0, 2), dq.transpose(2, 0, 1), gc, uv.reshape(NH, DL, VH)
 

time: 153 us -> 133 us (0.87)
  Pallas kernels: 137 us -> 122 us
  local copies, waits for them, and re-layouts: 13.3 us -> 10.5 us
  other arithmetic: 1.89 us -> 0 us
    pallas_call x1, Pallas kernels: 137 us -> 122 us  [attention(): pl.pallas_call(fused_body, out_shape=(jax.ShapeDtypeStruct((NH, TD, VH),...]
    unnamed x9 -> x8, local copies, waits for them, and re-layouts: 13.1 us -> 10.5 us
where the time goes in v3:
time: 133 us
  Pallas kernels  122 us (92%)
  local copies, waits for them, and re-layouts  10.5 us (8%)
    pallas_call x1, Pallas kernels, attention(): pl.pallas_call(fused_body, out_shape=(jax.ShapeDtypeStruct((NH, TD, VH),...  122 us
    unnamed x8, local copies, waits for them, and re-layouts  10.5 us

profile of v3, /device:TPU:1, one launch (start us, length us, event | category | flops | bytes accessed | tf_op | source)
XLA Modules:
  0.0 133.0 jit_solution(9866550307166908915)
XLA Ops:
  0.6 121.9 %latent_attention.1 = (bf16[32,128,128]{2,1,0:T(8,128)(2,1)}, bf16[32,576,128]{2,1,0:T(8,128)(2,1)}, bf16[4,4096,128]{2,1,0:T(8,128)(2,1)}, f32[32,576]{1,0:T(8,128)}) custom-call(s32[2,15]{1,0:T(2,128)} %lists.1, bf16[32,576]{1,0:T(8,128)(2,1)} %cache.1, bf16[32,576,128]{2,1,0:T(8,128)(2,1)} %bitcast.5, bf16[32,512,128]{2,1,0:T(8,128)(2,1)} %w_hbm.1, ...), custom_call_target="tpu_custom_call" | custom-call | tf_op jit(solution)/shard_map/latent_attention/pallas_call | solution.py:769
  122.5 2.9 %copy.9 = bf16[128,32,128]{2,1,0:T(8,128)(2,1)} copy(bf16[128,32,128]{2,0,1:T(8,128)(2,1)} %bitcast.9) | data formatting | bytes 2097152
  125.4 0.0 copy-start.1
  125.4 0.0 copy-start
  125.4 5.0 %copy.13 = bf16[128,32,576]{0,2,1:T(8,128)(2,1)} copy(bf16[128,32,576]{0,2,1:T(8,128)(2,1)} %bitcast.6) | data formatting | bytes 9437184
  130.4 0.0 copy-done.1
  130.4 0.6 copy.14
  131.0 0.0 copy-done
  131.0 2.0 %copy.15 = bf16[32,512,128]{2,1,0:T(8,128)(2,1)} copy(bf16[32,512,128]{2,1,0:T(8,128)(2,1)S(1)} %bitcast.7) | data formatting | bytes 8388608
Async XLA Ops:
  125.4 5.0 %copy-start.1 = (f32[32,576]{1,0:T(8,128)S(1)}, f32[32,576]{1,0:T(8,128)}, u32[]{:S(2)}) copy-start(f32[32,576]{1,0:T(8,128)} %get-tuple-element.22) | copy-start | bytes 221188
  125.4 5.6 %copy-start = (bf16[4,4096,128]{2,1,0:T(8,128)(2,1)S(1)}, bf16[4,4096,128]{2,1,0:T(8,128)(2,1)}, u32[]{:S(2)}) copy-start(bf16[4,4096,128]{2,1,0:T(8,128)(2,1)} %get-tuple-element.11) | copy-start | bytes 12582916

commit v4 on v3

--- a/solution.py
+++ b/solution.py
@@ -310,14 +310,14 @@
     def step4(self):
         for a in (-1, 1):
             self.b_relay(a)
+
+    def step5(self):
         for a in (-1, 1):
             self.b_rest(a)
-
-    def step5(self):
         self.b_relay(2)
+
+    def step6(self):
         self.b_rest(2)
-
-    def step6(self):
         for a in (0, -1, 1, 2):
             k = a % 4
             self.got(self.at(a, 2, 0), self.r4.at[k, 0])
@@ -435,9 +435,10 @@
     pltpu.SemaphoreType.DMA((3,)),
 ]
 
-PHASES = [("fwd", 8, 2.3), ("ds0", 2, 1.3), ("kv0", 2, 2.6), ("ds1", 2, 1.3), ("kv1", 2, 2.6), ("dq", 4, 1.5)]
-UV_GAP = 3.2
-HEAD_GAP = 4.0
+PHASES = [("fwd", 8, 2.3), ("ds0", 2, 1.3), ("kv0", 4, 1.3), ("ds1", 2, 1.3), ("kv1", 4, 1.3), ("dq", 4, 1.5)]
+UV_GAPS = [0.0, 2.6, 2.4, 3.4, 1.8, 2.0, 2.0, 1.8, 3.4, 2.4, 2.6]
+HEAD_GAPS = [3.0, 4.0]
+END_GAPS = [0.1, 10.0, 2.5]
 
 
 def plan():
@@ -449,14 +450,19 @@
     when = {(name, i): t for t, name, i in ends}
     todo = []
     for k in range(NCH):
-        ready = when["fwd", 8 // NCH * (k + 1) - 1]
+        t = when["fwd", 8 // NCH * (k + 1) - 1]
         for st in range(11):
-            todo.append((ready + st * UV_GAP, "uv", (k, st)))
+            t += UV_GAPS[st]
+            todo.append((t, "uv", (k, st)))
     for u in range(4):
-        ready = when["kv%d" % (u // 2), u % 2]
-        todo.append((ready, "head_send", (u,)))
-        todo.append((ready + HEAD_GAP, "head_relay", (u,)))
-        todo.append((ready + 2 * HEAD_GAP, "head_sum", (u,)))
+        t = when["kv%d" % (u // 2), 2 * (u % 2) + 1]
+        todo.append((t, "head_send", (u,)))
+        todo.append((t + HEAD_GAPS[0], "head_relay", (u,)))
+        t += sum(HEAD_GAPS)
+        todo.append((t, "head_sum", (u,)))
+    for op, gap in zip(("spread", "collect", "finish"), END_GAPS):
+        t += gap
+        todo.append((t, op, ()))
     todo.sort(key=lambda e: e[0])
     at, late = {}, []
     for t, op, arg in todo:
@@ -530,6 +536,7 @@
         return 0
 
     lax.fori_loop(0, TD // 16, turn, 0)
+    lax.fori_loop(0, 32, find, 0)
     gat.step1()
 
     def prep_q(lo, hi):
@@ -565,14 +572,14 @@
 
     prep_q(0, 2)
     gat.step2()
-    prep_q(2, 4)
+    prep_q(2, 3)
     gat.step3()
+    prep_q(3, 4)
+    gat.step4()
     w_load.wait()
     prep_do(0, 2)
-    gat.step4()
+    gat.step5()
     prep_do(2, 4)
-    gat.step5()
-    lax.fori_loop(0, 32, find, 0)
     gat.step6()
     gat.step7()
 
@@ -601,7 +608,9 @@
             if arg[1] == 10:
                 uv_out[arg[0]].start()
         else:
-            {"head_send": head_send, "head_relay": head_relay, "head_sum": head_sum}[op](*arg)
+            ops = {"head_send": head_send, "head_relay": head_relay, "head_sum": head_sum}
+            ops.update({"spread": spread, "collect": collect, "finish": finish})
+            ops[op](*arg)
 
     at, late = plan()
     steps = {p[0]: p[1] for p in PHASES}
@@ -695,6 +704,7 @@
         def body(i):
             rows = cols(i)
             sa[:KV] = lax.dot_general(qg[g, :KV, :], pt[d, rows, :], NTD, preferred_element_type=F32)
+            hook("kv%d" % g, i, 0, 2)
             sb[:DL] = lax.dot_general(do[g], pt[g, rows, :], NTD, preferred_element_type=F32)
             zero = jnp.zeros((KP - KV, WIDE), F32)
             t = jnp.concatenate([sa[:DL] * SC + sb[:DL], sa[DL:KV] * SC, zero], 0).astype(BF)
@@ -704,9 +714,9 @@
         return body
 
     loop("ds0", back_ds(0, 2))
-    loop("kv0", back_kv(0, 2))
+    loop("kv0", back_kv(0, 2), 2)
     loop("ds1", back_ds(1, 0))
-    loop("kv1", back_kv(1, 0))
+    loop("kv1", back_kv(1, 0), 2)
 
     def dq_store(i, slot):
         return pltpu.make_async_copy(qb.at[slot], dq_hbm.at[pl.ds(8 * i, 8)], qsem.at[slot])
@@ -730,9 +740,6 @@
     loop("dq", back_q)
     for op, arg in late:
         run(op, arg)
-    spread()
-    collect()
-    finish()
     dq_store(2, 0).wait()
     dq_store(3, 1).wait()
     for q in uv_out:

time: 133 us -> 130 us (0.977)
  Pallas kernels: 122 us -> 119 us
    pallas_call x1, Pallas kernels: 122 us -> 119 us  [attention(): pl.pallas_call(fused_body, out_shape=(jax.ShapeDtypeStruct((NH, TD, VH),...]
where the time goes in v4:
time: 130 us
  Pallas kernels  119 us (92%)
  local copies, waits for them, and re-layouts  10.5 us (8%)
    pallas_call x1, Pallas kernels, attention(): pl.pallas_call(fused_body, out_shape=(jax.ShapeDtypeStruct((NH, TD, VH),...  119 us
    unnamed x8, local copies, waits for them, and re-layouts  10.5 us

profile of v4, /device:TPU:1, one launch (start us, length us, event | category | flops | bytes accessed | tf_op | source)
XLA Modules:
  0.0 129.9 jit_solution(5599066644296155809)
XLA Ops:
  0.6 118.8 %latent_attention.1 = (bf16[32,128,128]{2,1,0:T(8,128)(2,1)}, bf16[32,576,128]{2,1,0:T(8,128)(2,1)}, bf16[4,4096,128]{2,1,0:T(8,128)(2,1)}, f32[32,576]{1,0:T(8,128)}) custom-call(s32[2,15]{1,0:T(2,128)} %lists.1, bf16[32,576]{1,0:T(8,128)(2,1)} %cache.1, bf16[32,576,128]{2,1,0:T(8,128)(2,1)} %bitcast.5, bf16[32,512,128]{2,1,0:T(8,128)(2,1)} %w_hbm.1, ...), custom_call_target="tpu_custom_call" | custom-call | tf_op jit(solution)/shard_map/latent_attention/pallas_call | solution.py:776
  119.4 2.9 %copy.9 = bf16[128,32,128]{2,1,0:T(8,128)(2,1)} copy(bf16[128,32,128]{2,0,1:T(8,128)(2,1)} %bitcast.9) | data formatting | bytes 2097152
  122.3 0.0 copy-start.1
  122.3 0.0 copy-start
  122.3 5.0 %copy.13 = bf16[128,32,576]{0,2,1:T(8,128)(2,1)} copy(bf16[128,32,576]{0,2,1:T(8,128)(2,1)} %bitcast.6) | data formatting | bytes 9437184
  127.3 0.0 copy-done.1
  127.3 0.6 copy.14
  127.9 0.0 copy-done
  127.9 2.0 %copy.15 = bf16[32,512,128]{2,1,0:T(8,128)(2,1)} copy(bf16[32,512,128]{2,1,0:T(8,128)(2,1)S(1)} %bitcast.7) | data formatting | bytes 8388608
Async XLA Ops:
  122.3 5.0 %copy-start.1 = (f32[32,576]{1,0:T(8,128)S(1)}, f32[32,576]{1,0:T(8,128)}, u32[]{:S(2)}) copy-start(f32[32,576]{1,0:T(8,128)} %get-tuple-element.22) | copy-start | bytes 221188
  122.3 5.6 %copy-start = (bf16[4,4096,128]{2,1,0:T(8,128)(2,1)S(1)}, bf16[4,4096,128]{2,1,0:T(8,128)(2,1)}, u32[]{:S(2)}) copy-start(bf16[4,4096,128]{2,1,0:T(8,128)(2,1)} %get-tuple-element.11) | copy-start | bytes 12582916

commit v5 on v4

--- a/solution.py
+++ b/solution.py
@@ -55,11 +55,12 @@
     pl.semaphore_wait(barrier, len(seq_steps) + len(head_steps))
 
 
-def uv_stages(u, o, rc, ra1, ra2, rb, rb1, rb2, ss, rs):
+def uv_stages(u, rc, ra, rb, ri, ss, rs):
     s, z, c, x, y = place()
     twin = seq_at(y, x, 1 - c)
     pa = x * (1 - c) + y * c
     pb = y * (1 - c) + x * c
+    base = c * CH
 
     def nbr_a(d):
         return seq_at((y + d * c) % 4, (x + d * (1 - c)) % 4, c)
@@ -70,131 +71,70 @@
     def ds(start, size):
         return pl.ds(pl.multiple_of(start, size), size)
 
-    def add(dst, dst_ix, terms):
+    def add(terms):
         t = terms[0][...].astype(F32)
         for r in terms[1:]:
             t = t + r[...].astype(F32)
-        dst[dst_ix] = t.astype(BF)
-
-    def pair(k, st, a, b, nbr):
-        return [
-            rcopy(a[0], a[1], ss.at[k, st, 0], rs.at[k, st, 0], nbr(1), z),
-            rcopy(b[0], b[1], ss.at[k, st, 1], rs.at[k, st, 1], nbr(-1), z),
-        ]
-
-    base = c * CH
-
-    def out(k, start, size):
-        return o.at[k, pl.ds(pl.multiple_of(start, size), size)]
-
-    def c0(k):
-        return [rcopy(u.at[k, ds((1 - c) * CH, CH)], rc.at[k], ss.at[k, 0, 0], rs.at[k, 0, 0], twin, z)]
-
-    def c1(k):
-        q = ((pa + 2) % 4) * QA
-        return pair(k, 1, (rc.at[k, ds(q, QA // 2)], ra1.at[k, 0]),
-                    (rc.at[k, ds(q + QA // 2, QA // 2)], ra1.at[k, 1]), nbr_a)
-
-    def c2(k):
-        return pair(k, 2, (rc.at[k, ds((pa + 1) % 4 * QA, QA)], ra2.at[k, 0]),
-                    (rc.at[k, ds((pa + 3) % 4 * QA, QA)], ra2.at[k, 1]), nbr_a)
-
-    def c3(k):
-        q = ((pb + 2) % 4) * QB
-        return pair(k, 3, (rb.at[k, ds(q, QB // 2)], rb1.at[k, 0]),
-                    (rb.at[k, ds(q + QB // 2, QB // 2)], rb1.at[k, 1]), nbr_b)
-
-    def c4(k):
-        return pair(k, 4, (rb.at[k, ds((pb + 1) % 4 * QB, QB)], rb2.at[k, 0]),
-                    (rb.at[k, ds((pb + 3) % 4 * QB, QB)], rb2.at[k, 1]), nbr_b)
-
-    def c5(k):
-        m = out(k, base + pa * QA + pb * QB, QB)
-        return pair(k, 5, (m, m), (m, m), nbr_b)
-
-    def c6(k):
-        lo = out(k, base + pa * QA + (pb + 3) % 4 * QB, QB // 2)
-        hi = out(k, base + pa * QA + (pb + 1) % 4 * QB + QB // 2, QB // 2)
-        return pair(k, 6, (lo, lo), (hi, hi), nbr_b)
-
-    def c7(k):
-        m = out(k, base + pa * QA, QA)
-        return pair(k, 7, (m, m), (m, m), nbr_a)
-
-    def c8(k):
-        lo = out(k, base + (pa + 3) % 4 * QA, QA // 2)
-        hi = out(k, base + (pa + 1) % 4 * QA + QA // 2, QA // 2)
-        return pair(k, 8, (lo, lo), (hi, hi), nbr_a)
-
-    def c9(k):
-        m = out(k, base, CH)
-        return [rcopy(m, m, ss.at[k, 9, 0], rs.at[k, 9, 0], twin, z)]
-
-    def got5(k):
-        return [out(k, base + pa * QA + (pb + 3) % 4 * QB, QB), out(k, base + pa * QA + (pb + 1) % 4 * QB, QB)]
-
-    def got6(k):
-        q = base + pa * QA + (pb + 2) % 4 * QB
-        return [out(k, q, QB // 2), out(k, q + QB // 2, QB // 2)]
-
-    def got7(k):
-        return [out(k, base + (pa + 3) % 4 * QA, QA), out(k, base + (pa + 1) % 4 * QA, QA)]
-
-    def got8(k):
-        q = base + (pa + 2) % 4 * QA
-        return [out(k, q, QA // 2), out(k, q + QA // 2, QA // 2)]
-
-    def got9(k):
-        return [out(k, (1 - c) * CH, CH)]
-
-    makers = [c0, c1, c2, c3, c4, c5, c6, c7, c8, c9]
-
-    def arrived(k, st):
-        if st in (0, 1, 2, 3, 4):
-            for q in makers[st](k):
-                q.wait_recv()
-        else:
-            for i, dst in enumerate({5: got5, 6: got6, 7: got7, 8: got8, 9: got9}[st](k)):
-                rcopy(dst, dst, ss.at[k, st, i], rs.at[k, st, i], twin, z).wait_recv()
-        for q in makers[st](k):
-            q.wait_send()
+        return t.astype(BF)
+
+    def quarter_a(k, q):
+        return u.at[k, ds(base + q % 4 * QA, QA)]
+
+    def quarter_b(k, q):
+        return u.at[k, ds(base + pa * QA + q % 4 * QB, QB)]
+
+    def half(k, h):
+        return u.at[k, ds(h * CH, CH)]
+
+    def copies(k, st):
+        if st == 0:
+            return [(half(k, 1 - c), rc.at[k], twin)]
+        if st == 1:
+            return [(rc.at[k, ds((pa + d) % 4 * QA, QA)], ra.at[k, d - 1], nbr_a(d)) for d in (1, 2, 3)]
+        if st == 2:
+            return [(rb.at[k, ds((pb + d) % 4 * QB, QB)], ri.at[k, d - 1], nbr_b(d)) for d in (1, 2, 3)]
+        if st == 3:
+            return [(quarter_b(k, pb), quarter_b(k, pb), nbr_b(d)) for d in (1, 2, 3)]
+        if st == 4:
+            return [(quarter_a(k, pa), quarter_a(k, pa), nbr_a(d)) for d in (1, 2, 3)]
+        return [(half(k, c), half(k, c), twin)]
+
+    def landed(k, st):
+        if st == 3:
+            return [quarter_b(k, pb + 4 - d) for d in (1, 2, 3)]
+        if st == 4:
+            return [quarter_a(k, pa + 4 - d) for d in (1, 2, 3)]
+        if st == 5:
+            return [half(k, 1 - c)]
+        return [q[1] for q in copies(k, st)]
 
     def stage(k, st):
         if st > 0:
-            arrived(k, st - 1)
+            for i, dst in enumerate(landed(k, st - 1)):
+                rcopy(dst, dst, ss.at[k, st - 1, i], rs.at[k, st - 1, i], twin, z).wait_recv()
+            for i, (src, dst, to) in enumerate(copies(k, st - 1)):
+                rcopy(src, dst, ss.at[k, st - 1, i], rs.at[k, st - 1, i], to, z).wait_send()
         if st == 1:
-            add(rc, (k,), [u.at[k, ds(base, CH)], rc.at[k]])
+            rc[k] = add([half(k, c), rc.at[k]])
         elif st == 2:
-            a = ds((pa + 1) % 4 * QA, QA // 2)
-            b = ds((pa + 3) % 4 * QA + QA // 2, QA // 2)
-            add(rc, (k, a), [rc.at[k, a], ra1.at[k, 0]])
-            add(rc, (k, b), [rc.at[k, b], ra1.at[k, 1]])
+            rb[k] = add([rc.at[k, ds(pa * QA, QA)]] + [ra.at[k, d] for d in range(3)])
         elif st == 3:
-            add(rb, (k,), [rc.at[k, ds(pa * QA, QA)], ra2.at[k, 0], ra2.at[k, 1]])
-        elif st == 4:
-            a = ds((pb + 1) % 4 * QB, QB // 2)
-            b = ds((pb + 3) % 4 * QB + QB // 2, QB // 2)
-            add(rb, (k, a), [rb.at[k, a], rb1.at[k, 0]])
-            add(rb, (k, b), [rb.at[k, b], rb1.at[k, 1]])
-        elif st == 5:
-            add(o, (k, ds(base + pa * QA + pb * QB, QB)),
-                [rb.at[k, ds(pb * QB, QB)], rb2.at[k, 0], rb2.at[k, 1]])
-        if st < 10:
-            for q in makers[st](k):
-                q.start()
+            quarter_b(k, pb)[...] = add([rb.at[k, ds(pb * QB, QB)]] + [ri.at[k, d] for d in range(3)])
+        if st < UV_STAGES - 1:
+            for i, (src, dst, to) in enumerate(copies(k, st)):
+                rcopy(src, dst, ss.at[k, st, i], rs.at[k, st, i], to, z).start()
 
     return stage
 
 
+UV_STAGES = 7
 UV_SCRATCH = [
     pltpu.VMEM((NCH, CH, 128), BF),
-    pltpu.VMEM((NCH, 2, QA // 2, 128), BF),
-    pltpu.VMEM((NCH, 2, QA, 128), BF),
+    pltpu.VMEM((NCH, 3, QA, 128), BF),
     pltpu.VMEM((NCH, QA, 128), BF),
-    pltpu.VMEM((NCH, 2, QB // 2, 128), BF),
-    pltpu.VMEM((NCH, 2, QB, 128), BF),
-    pltpu.SemaphoreType.DMA((NCH, 10, 2)),
-    pltpu.SemaphoreType.DMA((NCH, 10, 2)),
+    pltpu.VMEM((NCH, 3, QB, 128), BF),
+    pltpu.SemaphoreType.DMA((NCH, UV_STAGES - 1, 3)),
+    pltpu.SemaphoreType.DMA((NCH, UV_STAGES - 1, 3)),
 ]
 
 
@@ -383,30 +323,52 @@
         if u % 2:
             rz[u // 2, 16] = jnp.zeros((16, KV), BF)
 
+    def packed(t):
+        v = rz[0, inv[0, t]].astype(F32) + rz[1, inv[1, t]].astype(F32)
+        mark = jnp.zeros((16, KP - KV), F32) + flag[t].astype(F32)
+        return jnp.concatenate([v, mark], 1).astype(BF)
+
+    def message(d):
+        return rcopy(send.at[d], recv.at[d], xss.at[d], xrs.at[d], (s + d) % 32, z)
+
     def spread():
-        for d in range(32):
-            t = (s + d) % 32
-            v = rz[0, inv[0, t]].astype(F32) + rz[1, inv[1, t]].astype(F32)
-            mark = jnp.zeros((16, KP - KV), F32) + flag[t].astype(F32)
-            send[d] = jnp.concatenate([v, mark], 1).astype(BF)
-            if d:
-                rcopy(send.at[d], recv.at[d], xss.at[d], xrs.at[d], t, z).start()
+        send[0] = packed(s)
+
+        def one(d, _):
+            @pl.when(s + d >= 32)
+            def _():
+                send[d] = packed((s + d) % 32)
+                message(d).start()
+
+            return 0
+
+        lax.fori_loop(1, 32, one, 0)
+
+    def take(v):
+        v = v.astype(F32)
+        v, mark = v[:, :KV], v[:, KV : KV + 1]
+        second_part = v * mark
+        part[0, 0] = part[0, 0] + (v - second_part)
+        part[0, 1] = part[0, 1] + second_part
 
     def collect():
-        a = jnp.zeros((16, KV), F32)
-        b = jnp.zeros((16, KV), F32)
-        for d in range(32):
-            if d:
-                rcopy(send.at[d], recv.at[d], xss.at[d], xrs.at[d], (s + d) % 32, z).wait()
-                v = recv[d].astype(F32)
-            else:
-                v = send[0].astype(F32)
-            v, mark = v[:, :KV], v[:, KV : KV + 1]
-            second_part = v * mark
-            b = b + second_part
-            a = a + (v - second_part)
-        part[0, 0] = a + rz[0, 0].astype(F32)
-        part[0, 1] = b + rz[1, 0].astype(F32)
+        part[0, 0] = rz[0, 0].astype(F32)
+        part[0, 1] = rz[1, 0].astype(F32)
+        take(send[0])
+
+        def one(d, _):
+            @pl.when(d > s)
+            def _():
+                message(d).wait_recv()
+                take(recv[d])
+
+            @pl.when(s + d >= 32)
+            def _():
+                message(d).wait_send()
+
+            return 0
+
+        lax.fori_loop(1, 32, one, 0)
         for d in (1, 2, 3):
             rcopy(part.at[0], part.at[d], fss.at[d - 1], frs.at[d - 1], s, (z + d) % 4).start()
 
@@ -436,9 +398,9 @@
 ]
 
 PHASES = [("fwd", 8, 2.3), ("ds0", 2, 1.3), ("kv0", 4, 1.3), ("ds1", 2, 1.3), ("kv1", 4, 1.3), ("dq", 4, 1.5)]
-UV_GAPS = [0.0, 2.6, 2.4, 3.4, 1.8, 2.0, 2.0, 1.8, 3.4, 2.4, 2.6]
+UV_GAPS = [0.0, 2.8, 4.6, 2.8, 2.8, 4.6, 2.8]
 HEAD_GAPS = [3.0, 4.0]
-END_GAPS = [0.1, 10.0, 2.5]
+END_GAPS = [0.1, 8.0, 2.5]
 
 
 def plan():
@@ -451,7 +413,7 @@
     todo = []
     for k in range(NCH):
         t = when["fwd", 8 // NCH * (k + 1) - 1]
-        for st in range(11):
+        for st in range(UV_STAGES):
             t += UV_GAPS[st]
             todo.append((t, "uv", (k, st)))
     for u in range(4):
@@ -482,7 +444,7 @@
     gat = Gather(cache, *scr[: len(GATHER_SCRATCH)])
     full = gat.full
     scr = scr[len(GATHER_SCRATCH) :]
-    stage = uv_stages(u, u, *scr[: len(UV_SCRATCH)])
+    stage = uv_stages(u, *scr[: len(UV_SCRATCH)])
     gk = full
     cs = cache_stages(inv, flag, gk, gc, *scr[len(UV_SCRATCH) :])
     head_send, head_relay, head_sum, spread, collect, finish = cs
@@ -605,7 +567,7 @@
     def run(op, arg):
         if op == "uv":
             stage(*arg)
-            if arg[1] == 10:
+            if arg[1] == UV_STAGES - 1:
                 uv_out[arg[0]].start()
         else:
             ops = {"head_send": head_send, "head_relay": head_relay, "head_sum": head_sum}

time: 130 us -> 121 us (0.931)
  Pallas kernels: 119 us -> 110 us
    pallas_call x1, Pallas kernels: 119 us -> 110 us  [attention(): pl.pallas_call(fused_body, out_shape=(jax.ShapeDtypeStruct((NH, TD, VH),...]
where the time goes in v5:
time: 121 us
  Pallas kernels  110 us (91%)
  local copies, waits for them, and re-layouts  10.5 us (9%)
    pallas_call x1, Pallas kernels, attention(): pl.pallas_call(fused_body, out_shape=(jax.ShapeDtypeStruct((NH, TD, VH),...  110 us
    unnamed x8, local copies, waits for them, and re-layouts  10.5 us

profile of v5, /device:TPU:1, one launch (start us, length us, event | category | flops | bytes accessed | tf_op | source)
XLA Modules:
  0.0 121.3 jit_solution(15507154499149680877)
XLA Ops:
  0.6 110.1 %latent_attention.1 = (bf16[32,128,128]{2,1,0:T(8,128)(2,1)}, bf16[32,576,128]{2,1,0:T(8,128)(2,1)}, bf16[4,4096,128]{2,1,0:T(8,128)(2,1)}, f32[32,576]{1,0:T(8,128)}) custom-call(s32[2,15]{1,0:T(2,128)} %lists.1, bf16[32,576]{1,0:T(8,128)(2,1)} %cache.1, bf16[32,576,128]{2,1,0:T(8,128)(2,1)} %bitcast.5, bf16[32,512,128]{2,1,0:T(8,128)(2,1)} %w_hbm.1, ...), custom_call_target="tpu_custom_call" | custom-call | tf_op jit(solution)/shard_map/latent_attention/pallas_call | solution.py:738
  110.7 2.9 %copy.9 = bf16[128,32,128]{2,1,0:T(8,128)(2,1)} copy(bf16[128,32,128]{2,0,1:T(8,128)(2,1)} %bitcast.9) | data formatting | bytes 2097152
  113.6 0.0 copy-start.1
  113.6 0.0 copy-start
  113.6 5.0 %copy.13 = bf16[128,32,576]{0,2,1:T(8,128)(2,1)} copy(bf16[128,32,576]{0,2,1:T(8,128)(2,1)} %bitcast.6) | data formatting | bytes 9437184
  118.6 0.0 copy-done.1
  118.6 0.6 copy.14
  119.2 0.0 copy-done
  119.3 2.0 %copy.15 = bf16[32,512,128]{2,1,0:T(8,128)(2,1)} copy(bf16[32,512,128]{2,1,0:T(8,128)(2,1)S(1)} %bitcast.7) | data formatting | bytes 8388608
Async XLA Ops:
  113.6 5.0 %copy-start.1 = (f32[32,576]{1,0:T(8,128)S(1)}, f32[32,576]{1,0:T(8,128)}, u32[]{:S(2)}) copy-start(f32[32,576]{1,0:T(8,128)} %get-tuple-element.22) | copy-start | bytes 221188
  113.6 5.6 %copy-start = (bf16[4,4096,128]{2,1,0:T(8,128)(2,1)S(1)}, bf16[4,4096,128]{2,1,0:T(8,128)(2,1)}, u32[]{:S(2)}) copy-start(bf16[4,4096,128]{2,1,0:T(8,128)(2,1)} %get-tuple-element.11) | copy-start | bytes 12582916

commit v6 on v5

--- a/solution.py
+++ b/solution.py
@@ -332,35 +332,27 @@
         return rcopy(send.at[d], recv.at[d], xss.at[d], xrs.at[d], (s + d) % 32, z)
 
     def spread():
-        send[0] = packed(s)
+        for d in range(32):
+            send[d] = packed((s + d) % 32)
 
         def one(d, _):
             @pl.when(s + d >= 32)
             def _():
-                send[d] = packed((s + d) % 32)
                 message(d).start()
 
             return 0
 
         lax.fori_loop(1, 32, one, 0)
 
-    def take(v):
-        v = v.astype(F32)
-        v, mark = v[:, :KV], v[:, KV : KV + 1]
-        second_part = v * mark
-        part[0, 0] = part[0, 0] + (v - second_part)
-        part[0, 1] = part[0, 1] + second_part
+    def last(b):
+        h = 2 * b + z // 2
+        return h, rcopy(part.at[b], part.at[2 + z % 2], fss.at[b], frs.at[z % 2], s, h)
 
     def collect():
-        part[0, 0] = rz[0, 0].astype(F32)
-        part[0, 1] = rz[1, 0].astype(F32)
-        take(send[0])
-
         def one(d, _):
             @pl.when(d > s)
             def _():
                 message(d).wait_recv()
-                take(recv[d])
 
             @pl.when(s + d >= 32)
             def _():
@@ -369,15 +361,44 @@
             return 0
 
         lax.fori_loop(1, 32, one, 0)
-        for d in (1, 2, 3):
-            rcopy(part.at[0], part.at[d], fss.at[d - 1], frs.at[d - 1], s, (z + d) % 4).start()
+        first = rz[0, 0].astype(F32)
+        other = rz[1, 0].astype(F32)
+        for d in range(32):
+            v = (recv[d] if d else send[0]).astype(F32)
+            if d:
+                v = jnp.where(d > s, v, 0.0)
+            v, mark = v[:, :KV], v[:, KV : KV + 1]
+            moved = v * mark
+            other = other + moved
+            first = first + (v - moved)
+        part[0] = first
+        part[1] = other
+        for b in range(2):
+            h, q = last(b)
+
+            @pl.when(h != z)
+            def _():
+                q.start()
 
     def finish():
-        for d in (1, 2, 3):
-            rcopy(part.at[0], part.at[d], fss.at[d - 1], frs.at[d - 1], s, (z + d) % 4).wait()
-        q = 2 * (z % 2)
-        gc[0:16] = part[(z - q + 4) % 4, z // 2]
-        gc[16:32] = part[(z - q + 3) % 4, z // 2]
+        for i in range(2):
+            src = 2 * (z % 2) + i
+
+            @pl.when(src == z)
+            def _():
+                gc[16 * i : 16 * i + 16] = part[z // 2]
+
+            @pl.when(src != z)
+            def _():
+                rcopy(part.at[2 + i], part.at[2 + i], fss.at[0], frs.at[i], s, (z + 1) % 4).wait_recv()
+                gc[16 * i : 16 * i + 16] = part[2 + i]
+
+        for b in range(2):
+            h, q = last(b)
+
+            @pl.when(h != z)
+            def _():
+                q.wait_send()
 
     return head_send, head_relay, head_sum, spread, collect, finish
 
@@ -388,13 +409,13 @@
     pltpu.VMEM((2, 17, 16, KV), BF),
     pltpu.VMEM((32, 16, KP), BF),
     pltpu.VMEM((32, 16, KP), BF),
-    pltpu.VMEM((4, 2, 16, KV), F32),
+    pltpu.VMEM((4, 16, KV), F32),
     pltpu.SemaphoreType.DMA((4, 2, 2)),
     pltpu.SemaphoreType.DMA((4, 2, 2)),
     pltpu.SemaphoreType.DMA((32,)),
     pltpu.SemaphoreType.DMA((32,)),
-    pltpu.SemaphoreType.DMA((3,)),
-    pltpu.SemaphoreType.DMA((3,)),
+    pltpu.SemaphoreType.DMA((2,)),
+    pltpu.SemaphoreType.DMA((2,)),
 ]
 
 PHASES = [("fwd", 8, 2.3), ("ds0", 2, 1.3), ("kv0", 4, 1.3), ("ds1", 2, 1.3), ("kv1", 4, 1.3), ("dq", 4, 1.5)]
@@ -753,11 +774,73 @@
     )(lists, cache, qt, w, gout)
 
 
+def hand_on_body(ho, dq, uv, gc, ho_out, dq_out, uv_out, gc_out, vh, vt, vq, vu, vg, si, so):
+    def part(ref, i):
+        return ref.at[pl.ds(8 * i, 8)]
+
+    gc_in = pltpu.make_async_copy(gc, vg, si.at[3, 0])
+    gc_copy = pltpu.make_async_copy(vg, gc_out, so.at[3, 0])
+    ins, outs = [], []
+    for i in range(4):
+        ins.append(pltpu.make_async_copy(part(ho, i), part(vh, i), si.at[0, i]))
+    for i in range(4):
+        ins.append(pltpu.make_async_copy(part(dq, i), part(vq, i), si.at[1, i]))
+        outs.append(pltpu.make_async_copy(part(vq, i), part(dq_out, i), so.at[1, i]))
+        ins.append(pltpu.make_async_copy(part(uv, i), part(vu, i), si.at[2, i]))
+        outs.append(pltpu.make_async_copy(part(vu, i), part(uv_out, i), so.at[2, i]))
+    gc_in.start()
+    for q in ins:
+        q.start()
+    gc_in.wait()
+    gc_copy.start()
+    for q in ins[:4]:
+        q.wait()
+    turns = []
+    for i in range(4):
+        for q, out in zip(ins[4 + 2 * i : 6 + 2 * i], outs[2 * i : 2 * i + 2]):
+            q.wait()
+            out.start()
+        t = pl.ds(32 * i, 32)
+        vt[t] = jnp.swapaxes(vh[:, t, :], 0, 1)
+        turns.append(pltpu.make_async_copy(vt.at[t], ho_out.at[t], so.at[0, i]))
+        turns[-1].start()
+    for q in outs + turns:
+        q.wait()
+    gc_copy.wait()
+
+
+def hand_on(ho, dq, uv, gc):
+    a = pl.BlockSpec(memory_space=pl.ANY)
+    return pl.pallas_call(
+        hand_on_body,
+        out_shape=(
+            jax.ShapeDtypeStruct((TD, NH, VH), BF),
+            jax.ShapeDtypeStruct((NH, KV, TD), BF),
+            jax.ShapeDtypeStruct((NH, DL, VH), BF),
+            jax.ShapeDtypeStruct((32, KV), F32),
+        ),
+        in_specs=[a] * 4,
+        out_specs=(a,) * 4,
+        scratch_shapes=[
+            pltpu.VMEM((NH, TD, VH), BF),
+            pltpu.VMEM((TD, NH, VH), BF),
+            pltpu.VMEM((NH, KV, TD), BF),
+            pltpu.VMEM((NH, DL, VH), BF),
+            pltpu.VMEM((32, KV), F32),
+            pltpu.SemaphoreType.DMA((4, 4)),
+            pltpu.SemaphoreType.DMA((4, 4)),
+        ],
+        compiler_params=pltpu.CompilerParams(vmem_limit_bytes=VMEM_LIMIT),
+        name="hand_on",
+    )(ho, dq, uv, gc)
+
+
 def on_device(queries, cache, lists, w_uv, grad_out):
     ho, dq, uv, gc = attention(
         lists, cache, queries.transpose(1, 2, 0), w_uv, grad_out.reshape(TD * NH, VH)
     )
-    return ho.transpose(1, 0, 2), dq.transpose(2, 0, 1), gc, uv.reshape(NH, DL, VH)
+    ho, dq, uv, gc = hand_on(ho, dq, uv.reshape(NH, DL, VH), gc)
+    return ho, dq.transpose(2, 0, 1), gc, uv
 
 
 def solution(mesh):

time: 121 us -> 114 us (0.942)
  local copies, waits for them, and re-layouts: 10.5 us -> 0 us
  Pallas kernels: 110 us -> 113 us
    unnamed x8 -> x0, local copies, waits for them, and re-layouts: 10.5 us -> none
    pallas_call x0 -> x1, Pallas kernels: none -> 7.7 us  [hand_on(): pl.pallas_call(hand_on_body, out_shape=(jax.ShapeDtypeStruct((TD, NH, VH)...]
    pallas_call x1, Pallas kernels: 110 us -> 105 us  [attention(): pl.pallas_call(fused_body, out_shape=(jax.ShapeDtypeStruct((NH, TD, VH),...]
where the time goes in v6:
time: 114 us
  Pallas kernels  113 us (99%)
    pallas_call x1, Pallas kernels, attention(): pl.pallas_call(fused_body, out_shape=(jax.ShapeDtypeStruct((NH, TD, VH),...  105 us
    pallas_call x1, Pallas kernels, hand_on(): pl.pallas_call(hand_on_body, out_shape=(jax.ShapeDtypeStruct((TD, NH, VH)...  7.7 us

profile of v6, /device:TPU:1, one launch (start us, length us, event | category | flops | bytes accessed | tf_op | source)
XLA Modules:
  0.0 113.7 jit_solution(413334343987050993)
XLA Ops:
  0.6 105.2 %latent_attention.1 = (bf16[32,128,128]{2,1,0:T(8,128)(2,1)}, bf16[32,576,128]{2,1,0:T(8,128)(2,1)}, bf16[4,4096,128]{2,1,0:T(8,128)(2,1)}, f32[32,576]{1,0:T(8,128)}) custom-call(s32[2,15]{1,0:T(2,128)} %lists.1, bf16[32,576]{1,0:T(8,128)(2,1)} %cache.1, bf16[32,576,128]{2,1,0:T(8,128)(2,1)} %bitcast.4, bf16[32,512,128]{2,1,0:T(8,128)(2,1)} %w_hbm.1, ...), custom_call_target="tpu_custom_call" | custom-call | tf_op jit(solution)/shard_map/latent_attention/pallas_call | solution.py:759
  105.9 7.7 %hand_on.1 = (bf16[128,32,128]{2,1,0:T(8,128)(2,1)}, bf16[32,576,128]{2,1,0:T(8,128)(2,1)}, bf16[32,512,128]{2,1,0:T(8,128)(2,1)}, f32[32,576]{1,0:T(8,128)}) custom-call(bf16[32,128,128]{2,1,0:T(8,128)(2,1)} %get-tuple-element.12.ho, bf16[32,576,128]{2,1,0:T(8,128)(2,1)} %get-tuple-element.13.dq, bf16[32,512,128]{2,1,0:T(8,128)(2,1)} %bitcast.5, ...), custom_call_target="tpu_custom_call" | custom-call | tf_op jit(solution)/shard_map/hand_on/pallas_call | solution.py:814

commit v7 on v6

--- a/solution.py
+++ b/solution.py
@@ -419,8 +419,8 @@
 ]
 
 PHASES = [("fwd", 8, 2.3), ("ds0", 2, 1.3), ("kv0", 4, 1.3), ("ds1", 2, 1.3), ("kv1", 4, 1.3), ("dq", 4, 1.5)]
-UV_GAPS = [0.0, 2.8, 4.6, 2.8, 2.8, 4.6, 2.8]
-HEAD_GAPS = [3.0, 4.0]
+UV_GAPS = [0.0, 4.8, 7.8, 4.8, 4.8, 7.8, 4.8]
+HEAD_GAPS = [5.1, 6.8]
 END_GAPS = [0.1, 8.0, 2.5]
 
 

time: 114 us -> 107 us (0.939)
  Pallas kernels: 113 us -> 106 us
    pallas_call x1, Pallas kernels: 105 us -> 98 us  [attention(): pl.pallas_call(fused_body, out_shape=(jax.ShapeDtypeStruct((NH, TD, VH),...]
where the time goes in v7:
time: 107 us; the launch traced here: 106 us
  Pallas kernels  106 us (99%)
    pallas_call x1, Pallas kernels, attention(): pl.pallas_call(fused_body, out_shape=(jax.ShapeDtypeStruct((NH, TD, VH),...  98 us
    pallas_call x1, Pallas kernels, hand_on(): pl.pallas_call(hand_on_body, out_shape=(jax.ShapeDtypeStruct((TD, NH, VH)...  7.7 us

profile of v7, /device:TPU:1, one launch (start us, length us, event | category | flops | bytes accessed | tf_op | source)
XLA Modules:
  0.0 106.5 jit_solution(10215131139431808677)
XLA Ops:
  0.6 98.0 %latent_attention.1 = (bf16[32,128,128]{2,1,0:T(8,128)(2,1)}, bf16[32,576,128]{2,1,0:T(8,128)(2,1)}, bf16[4,4096,128]{2,1,0:T(8,128)(2,1)}, f32[32,576]{1,0:T(8,128)}) custom-call(s32[2,15]{1,0:T(2,128)} %lists.1, bf16[32,576]{1,0:T(8,128)(2,1)} %cache.1, bf16[32,576,128]{2,1,0:T(8,128)(2,1)} %bitcast.4, bf16[32,512,128]{2,1,0:T(8,128)(2,1)} %w_hbm.1, ...), custom_call_target="tpu_custom_call" | custom-call | tf_op jit(solution)/shard_map/latent_attention/pallas_call | solution.py:759
  98.6 7.7 %hand_on.1 = (bf16[128,32,128]{2,1,0:T(8,128)(2,1)}, bf16[32,576,128]{2,1,0:T(8,128)(2,1)}, bf16[32,512,128]{2,1,0:T(8,128)(2,1)}, f32[32,576]{1,0:T(8,128)}) custom-call(bf16[32,128,128]{2,1,0:T(8,128)(2,1)} %get-tuple-element.12.ho, bf16[32,576,128]{2,1,0:T(8,128)(2,1)} %get-tuple-element.13.dq, bf16[32,512,128]{2,1,0:T(8,128)(2,1)} %bitcast.5, ...), custom_call_target="tpu_custom_call" | custom-call | tf_op jit(solution)/shard_map/hand_on/pallas_call | solution.py:814

commit v8 on v7

--- a/solution.py
+++ b/solution.py
@@ -421,7 +421,7 @@
 PHASES = [("fwd", 8, 2.3), ("ds0", 2, 1.3), ("kv0", 4, 1.3), ("ds1", 2, 1.3), ("kv1", 4, 1.3), ("dq", 4, 1.5)]
 UV_GAPS = [0.0, 4.8, 7.8, 4.8, 4.8, 7.8, 4.8]
 HEAD_GAPS = [5.1, 6.8]
-END_GAPS = [0.1, 8.0, 2.5]
+END_GAPS = [0.1, 13.6, 4.3]
 
 
 def plan():

time: 107 us -> 107 us (level)
  no operation moved by 1% of the time
where the time goes in v8:
time: 107 us; the launch traced here: 106 us
  Pallas kernels  106 us (99%)
    pallas_call x1, Pallas kernels, attention(): pl.pallas_call(fused_body, out_shape=(jax.ShapeDtypeStruct((NH, TD, VH),...  98 us
    pallas_call x1, Pallas kernels, hand_on(): pl.pallas_call(hand_on_body, out_shape=(jax.ShapeDtypeStruct((TD, NH, VH)...  7.7 us

profile of v8, /device:TPU:1, one launch (start us, length us, event | category | flops | bytes accessed | tf_op | source)
XLA Modules:
  0.0 106.5 jit_solution(10215131139431808677)
XLA Ops:
  0.6 98.0 %latent_attention.1 = (bf16[32,128,128]{2,1,0:T(8,128)(2,1)}, bf16[32,576,128]{2,1,0:T(8,128)(2,1)}, bf16[4,4096,128]{2,1,0:T(8,128)(2,1)}, f32[32,576]{1,0:T(8,128)}) custom-call(s32[2,15]{1,0:T(2,128)} %lists.1, bf16[32,576]{1,0:T(8,128)(2,1)} %cache.1, bf16[32,576,128]{2,1,0:T(8,128)(2,1)} %bitcast.4, bf16[32,512,128]{2,1,0:T(8,128)(2,1)} %w_hbm.1, ...), custom_call_target="tpu_custom_call" | custom-call | tf_op jit(solution)/shard_map/latent_attention/pallas_call | solution.py:759
  98.6 7.7 %hand_on.1 = (bf16[128,32,128]{2,1,0:T(8,128)(2,1)}, bf16[32,576,128]{2,1,0:T(8,128)(2,1)}, bf16[32,512,128]{2,1,0:T(8,128)(2,1)}, f32[32,576]{1,0:T(8,128)}) custom-call(bf16[32,128,128]{2,1,0:T(8,128)(2,1)} %get-tuple-element.12.ho, bf16[32,576,128]{2,1,0:T(8,128)(2,1)} %get-tuple-element.13.dq, bf16[32,512,128]{2,1,0:T(8,128)(2,1)} %bitcast.5, ...), custom_call_target="tpu_custom_call" | custom-call | tf_op jit(solution)/shard_map/hand_on/pallas_call | solution.py:814
